TPU v7x, 512 devices: a whole 4x4x16 slice. The times are simulated.
512 devices in a mesh: rows: 128 (over x, z, core), comp: 4 (over y).
Axes of the slice: x: 4, y: 4, z: 16, core: 2. Of those that a mesh axis runs over, the one named last changes fastest.
Arguments:
- frechet: float32 [4, 512, 8, 128, 128], P('comp', 'rows'), may hold values from -0.09375 to 0.09375
- pattern: int32 [512, 8], P('rows'), may hold values from 0 to 2047, as said below
- ownership: int32 [2048], replicated, may hold values from 0 to 2047, as said below
- seismograms: float32 [4, 65536], P(None, 'rows'), may hold values from -6 to 6
- signs: int32 [4, 65536], P(None, 'rows'), may hold values from 0 to 1
Outputs:
- model: float32 [4, 262144], P('comp', 'rows')
- data_dir: float32 [65536], P('rows')
Inputs may be any that keep to these rules, and one draw needn't show every extreme that they name: `pattern`: each row block names 8 different column blocks, and every column block is named by some row block. Slot s belongs to index s // 16 of rows. The stored blocks of the row blocks of one index of rows fall in groups of 4 consecutive ones (within a row block) whose slots belong to one index of rows; the groups of one index of rows go to different indices, so each index sends exactly 4 stored blocks to each of 8 indices and none to the others, and each index of rows receives from exactly 8 indices. `ownership`: each slot appears once.
All inputs are finite; a program needn't handle non-finite values.
Results may differ from a plain program's by a relative error of at most 0.0003.
Values sent between devices are 32-bit elements; how exact they have to be, the bound alone decides.
No kernel may reach another device: no remote copies, remote signals or barrier semaphores. Data moves between devices by JAX's collectives and lax.ppermute only.
A program may use at most 64 MiB of HBM per device.

v0:
```python
import jax
import jax.numpy as jnp
from jax import lax
from jax.sharding import PartitionSpec as P

ITERS = 2


EPS = 1e-12


def on_device(frechet, pattern, ownership, seismograms, signs):
    blocks = frechet[0]
    row_blocks = blocks.shape[0]
    stored = blocks.shape[1]
    width = blocks.shape[2]
    column_blocks = ownership.shape[0]
    peers = lax.axis_size("rows")
    owned_blocks = column_blocks // peers
    entries = row_blocks * stored
    signed = (2 * signs - 1).astype(jnp.float32)
    data = jnp.sum(signed * seismograms, axis=0)
    flat_ids = pattern.reshape(-1)
    matches = flat_ids[:, None] == lax.broadcasted_iota(jnp.int32, (1, column_blocks), 1)
    slot = jnp.sum(jnp.where(matches, ownership[None, :], 0), axis=1)

    def data_norm(values):
        return jnp.sqrt(lax.psum(jnp.sum(values * values), "rows") + EPS)

    def adjoint_terms(data_vec):
        terms = jnp.einsum(
            "rkij,ri->rkj",
            blocks,
            data_vec.reshape(row_blocks, width),
            precision=lax.Precision.HIGHEST,
        )
        return terms.reshape(entries, width)

    def adjoint(data_vec):
        terms = adjoint_terms(data_vec)
        targets = lax.broadcasted_iota(jnp.int32, (owned_blocks * lax.axis_size("rows"), 1), 0)
        select = (targets == slot[None, :]).astype(jnp.float32)
        return lax.psum_scatter(
            jnp.dot(select, terms, precision=lax.Precision.HIGHEST),
            "rows",
            scatter_dimension=0,
            tiled=True,
        ).reshape(-1)

    def model_norm(values):
        return jnp.sqrt(lax.psum(jnp.sum(values * values), ("rows", "comp")) + EPS)

    beta = data_norm(data)
    u_vec = data / beta
    v_vec = adjoint(u_vec)
    alpha = model_norm(v_vec)
    v_vec = v_vec / alpha
    w_vec = v_vec
    model = jnp.zeros_like(v_vec)
    phibar = beta
    rhobar = alpha
    for step in range(ITERS):
        piece = lax.all_gather(v_vec.reshape(owned_blocks, width), "rows", axis=0, tiled=True)
        columns = lax.broadcasted_iota(jnp.int32, (1, piece.shape[0]), 1)
        pick_select = (slot[:, None] == columns).astype(jnp.float32)
        forward_chosen = jnp.dot(pick_select, piece, precision=lax.Precision.HIGHEST)
        partial_rows = jnp.einsum(
            "rkij,rkj->ri",
            blocks,
            forward_chosen.reshape(row_blocks, stored, width),
            precision=lax.Precision.HIGHEST,
        )
        u_vec = lax.psum(partial_rows.reshape(-1), "comp") - alpha * u_vec
        beta = data_norm(u_vec)
        u_vec = u_vec / beta
        v_vec = adjoint(u_vec) - beta * v_vec
        alpha = model_norm(v_vec)
        v_vec = v_vec / alpha
        rho = jnp.sqrt(rhobar * rhobar + beta * beta)
        cosine = rhobar / rho
        sine = beta / rho
        theta = sine * alpha
        rhobar = -cosine * alpha
        phi = cosine * phibar
        phibar = sine * phibar
        model = model + phi / rho * w_vec
        w_vec = v_vec - theta / rho * w_vec
    return (model[None, :], u_vec)


def solution(mesh):
    placed = (
        P("comp", "rows", None, None, None),
        P("rows", None),
        P(),
        P(None, "rows"),
        P(None, "rows"),
    )
    return jax.shard_map(
        on_device,
        mesh=mesh,
        in_specs=placed,
        out_specs=(P("comp", "rows"), P("rows")),
        check_vma=False,
    )
```

profile of v0, /device:TPU:1, one launch (start us, length us, event | category | flops | bytes accessed | tf_op | source)
XLA Modules:
  0.0 1768.1 jit_solution(13732427576936283933)
XLA Ops:
  7.2 0.9 multiply_reduce_fusion.2
  8.1 0.6 multiply_reduce_fusion.5
  8.7 255.0 %psum.49 = f32[]{:T(128)} all-reduce(f32[]{:T(128)} %multiply_reduce_fusion.5), channel_id=1, replica_groups=mesh['rows'=128,'comp'=4] {'rows'}, use_global_device_ids=true, to_apply=%region_3.4 | all-reduce | flops 1 | bytes 8 | tf_op jit(solution)/shard_map/psum | solution.py:28
  264.4 0.8 eq.21
  265.2 1.1 fusion.6
  266.3 0.2 select_reduce_fusion
  266.5 1.6 fusion.9
  268.2 242.6 %reduce-scatter.3.cloned.1.call-done = f32[16,128]{1,0:T(8,128)} async-done(((f32[2048,128]{1,0:T(8,128)}), f32[16,128]{1,0:T(8,128)}) %reduce-scatter.3.cloned.1.call-update) | async-done | bytes 8208 | tf_op jit(solution)/shard_map/reduce_scatter | solution.py:43
  510.8 1.3 multiply_reduce_fusion.1
  512.1 112.8 %psum.50 = f32[]{:T(128)} all-reduce(f32[]{:T(128)} %multiply_reduce_fusion.1), channel_id=1, replica_groups=mesh['rows'=128,'comp'=4] {'rows','comp'}, use_global_device_ids=true, to_apply=%region_6.7 | all-reduce | flops 1 | bytes 8 | tf_op jit(solution)/shard_map/psum | solution.py:51
  625.6 1.3 broadcast_divide_fusion.1
  626.9 0.0 reduce-scatter.5.cloned.1.call-start
  627.0 125.9 %all-gather.3.cloned.1.call-done = f32[2048,128]{1,0:T(8,128)} async-done(((f32[16,128]{1,0:T(8,128)}), f32[2048,128]{1,0:T(8,128)}) %all-gather.3.cloned.1.call-update) | async-done | bytes 1048592 | tf_op jit(solution)/shard_map/all_gather | solution.py:63
  752.9 1.7 fusion.13
  754.6 1.8 fusion.4
  756.5 8.4 psum.51
  764.9 0.6 multiply_reduce_fusion.4
  765.5 249.1 %psum.52 = f32[]{:T(128)} all-reduce(f32[]{:T(128)} %multiply_reduce_fusion.4), channel_id=1, replica_groups=mesh['rows'=128,'comp'=4] {'rows'}, use_global_device_ids=true, to_apply=%region_9.10 | all-reduce | flops 1 | bytes 8 | tf_op jit(solution)/shard_map/psum | solution.py:28
  1015.3 1.1 fusion.2
  1016.4 1.6 fusion.8
  1018.1 237.7 %reduce-scatter.5.cloned.1.call-done = f32[16,128]{1,0:T(8,128)} async-done(((f32[2048,128]{1,0:T(8,128)}), f32[16,128]{1,0:T(8,128)}) %reduce-scatter.5.cloned.1.call-update) | async-done | bytes 8208 | tf_op jit(solution)/shard_map/reduce_scatter | solution.py:43
  1255.8 1.3 multiply_reduce_fusion
  1257.1 112.8 %psum.53 = f32[]{:T(128)} all-reduce(f32[]{:T(128)} %multiply_reduce_fusion), channel_id=1, replica_groups=mesh['rows'=128,'comp'=4] {'rows','comp'}, use_global_device_ids=true, to_apply=%region_12.13 | all-reduce | flops 1 | bytes 8 | tf_op jit(solution)/shard_map/psum | solution.py:51
  1370.5 1.3 broadcast_divide_fusion
  1372.1 125.7 %all-gather.5.cloned.1.call-done = f32[2048,128]{1,0:T(8,128)} async-done(((f32[16,128]{1,0:T(8,128)}), f32[2048,128]{1,0:T(8,128)}) %all-gather.5.cloned.1.call-update) | async-done | bytes 1048592 | tf_op jit(solution)/shard_map/all_gather | solution.py:63
  1497.8 1.7 fusion.12
  1499.6 1.8 fusion
  1501.4 8.4 psum.54
  1509.8 0.6 multiply_reduce_fusion.3
  1510.4 249.1 %psum.55 = f32[]{:T(128)} all-reduce(f32[]{:T(128)} %multiply_reduce_fusion.3), channel_id=1, replica_groups=mesh['rows'=128,'comp'=4] {'rows'}, use_global_device_ids=true, to_apply=%region_15.16 | all-reduce | flops 1 | bytes 8 | tf_op jit(solution)/shard_map/psum | solution.py:28
  1760.2 0.6 broadcast_divide_fusion.2
  1760.9 0.6 multiply_add_fusion
  (17 shorter events, 0.2 us)
Async XLA Ops:
  7.2 258.0 %copy-start = (f32[1,4,8,128,128]{4,3,2,1,0:T(8,128)S(1)}, f32[1,4,8,128,128]{4,3,2,1,0:T(8,128)}, u32[]{:S(2)}) copy-start(f32[1,4,8,128,128]{4,3,2,1,0:T(8,128)} %param.5) | copy-start | bytes 6291460
  7.2 259.1 %copy-start.3 = (s32[2048]{0:T(1024)S(1)}, s32[2048]{0:T(1024)}, u32[]{:S(2)}) copy-start(s32[2048]{0:T(1024)} %param.7) | copy-start | bytes 24580
  7.2 503.6 %reduce-scatter.3.cloned.1.call-start = ((), (), s32[]{:S(2)}) async-start(), calls=%async_computation.2 | async-start | bytes 1056768 | tf_op jit(solution)/shard_map/reduce_scatter | solution.py:43
  268.1 484.8 %all-gather.3.cloned.1.call-start = ((), (), s32[]{:S(2)}) async-start(), calls=%async_computation.3 | async-start | bytes 1056768 | tf_op jit(solution)/shard_map/all_gather | solution.py:63
  626.9 628.9 %reduce-scatter.5.cloned.1.call-start = ((), (), s32[]{:S(2)}) async-start(), calls=%async_computation.4 | async-start | bytes 1056768 | tf_op jit(solution)/shard_map/reduce_scatter | solution.py:43
  1015.3 240.5 %copy-start.1 = (f32[16,128]{1,0:T(8,128)S(1)}, f32[16,128]{1,0:T(8,128)}, u32[]{:S(2)}) copy-start(f32[16,128]{1,0:T(8,128)} %reduce-scatter.3.cloned.1.call-done) | copy-start | bytes 24580
  1018.0 479.8 %all-gather.5.cloned.1.call-start = ((), (), s32[]{:S(2)}) async-start(), calls=%async_computation.5 | async-start | bytes 1056768 | tf_op jit(solution)/shard_map/all_gather | solution.py:63
  1371.8 389.1 %copy-start.2 = (f32[16,128]{1,0:T(8,128)S(1)}, f32[16,128]{1,0:T(8,128)}, u32[]{:S(2)}) copy-start(f32[16,128]{1,0:T(8,128)} %broadcast_divide_fusion) | copy-start | bytes 24580
Sparse Core Ops, SparseCore 0:
  268.3 242.5 reduce-scatter.2
  627.0 125.8 all-gather.2
  1018.1 237.5 reduce-scatter.4
  1372.0 125.8 all-gather.4
where the time goes:
time: 1770 us
  blocking collectives  996 us (56%)
  waiting for transfers between devices  732 us (41%)
  between operations  17.7 us (1%)
    psum x3, blocking collectives, data_norm(): return jnp.sqrt(lax.psum(jnp.sum(values * values), 'rows') + EPS)  753 us
    reduce_scatter x2, waiting for transfers between devices, adjoint(): lax.psum_scatter(jnp.dot(select, terms, precision=lax.Precision.HIGHEST),...  480 us
    all_gather x2, waiting for transfers between devices, on_device(): lax.all_gather(v_vec.reshape(owned_blocks, width), 'rows', axis=0, tiled=...  252 us
    psum x2, blocking collectives, model_norm(): return jnp.sqrt(lax.psum(jnp.sum(values * values), ('rows', 'comp')) + EPS)  226 us
  transfers between devices with their start and end apart: 4, of which 4 were waited for; matrix products, arithmetic and copies ran while one was open for 0% of the time, Pallas kernels for 0%

commit v1 on v0

v1 whole, which is shorter than its diff:
```python
import jax
import jax.numpy as jnp
from jax import lax
from jax.experimental import pallas as pl
from jax.experimental.pallas import tpu as pltpu
from jax.sharding import Mesh
from jax.sharding import PartitionSpec as P

EPS = 1e-12
F32 = jnp.float32
BF16 = jnp.bfloat16

X, Z, CORE, Y = 4, 16, 2, 4
ROWS = ("x", "z", "core")
PLANE = ("x", "core")
N_PLANE = X * CORE
N_ROWS = X * Z * CORE

BS = 128
RB = 4
NNZ = 8
ENTRIES = RB * NNZ
OWN = 16
WANT = ENTRIES + OWN
ZCH = ENTRIES + 1
PCH = WANT + 8
GROUPS = BS // ENTRIES
DOTS = 9

VMEM = pl.BlockSpec(memory_space=pltpu.VMEM)
SMEM = pl.BlockSpec(memory_space=pltpu.SMEM)


def call(kernel, outs, ins, scratch=(), flops=0, moved=0):
    return pl.pallas_call(
        kernel,
        out_shape=tuple(jax.ShapeDtypeStruct(s, F32) for s in outs),
        in_specs=list(ins),
        out_specs=tuple(VMEM for _ in outs),
        scratch_shapes=list(scratch),
        compiler_params=pltpu.CompilerParams(vmem_limit_bytes=32 * 1024 * 1024),
        cost_estimate=pl.CostEstimate(flops=flops, bytes_accessed=moved, transcendentals=0),
    )


def two_sum(a, b):
    s = a + b
    bb = s - a
    return s, (a - (s - bb)) + (b - bb)


def halves(a):
    c = a * 4097.0
    high = c - (c - a)
    return high, a - high


def two_prod(a, b):
    p = a * b
    ah, al = halves(a)
    bh, bl = halves(b)
    return p, ((ah * bh - p) + ah * bl + al * bh) + al * bl


def dd_add(a, b):
    s, e = two_sum(a[0], b[0])
    e = e + (a[1] + b[1])
    h = s + e
    return h, e - (h - s)


def dd_mul(a, b):
    p, e = two_prod(a[0], b[0])
    e = e + (a[0] * b[1] + a[1] * b[0])
    h = p + e
    return h, e - (h - p)


def dd_scale(a, f):
    return a[0] * f, a[1] * f


def fold_rows(pair):
    n = pair[0].shape[0]
    while n > 1:
        n //= 2
        pair = dd_add((pair[0][:n], pair[1][:n]), (pair[0][n:], pair[1][n:]))
    return pair


def dot_rows(a, b):
    return fold_rows(two_prod(a, b))


def ids_kernel(pat, own, me, bmsg, idrow):
    sub = lax.broadcasted_iota(jnp.int32, (ENTRIES, BS), 0)
    lane = lax.broadcasted_iota(jnp.int32, (8, BS), 1) - me[1] * ENTRIES
    col = jnp.zeros((ENTRIES, BS), jnp.int32)
    row = jnp.full((8, BS), -1, jnp.int32)
    for e in range(ENTRIES):
        s = own[pat[e]]
        col = jnp.where(sub == e, s, col)
        row = jnp.where(lane == e, s, row)
    mine = me[0] * OWN + lax.broadcasted_iota(jnp.int32, (OWN, BS), 0)
    col = col.astype(F32)
    mine = mine.astype(F32)
    for i in range(N_PLANE):
        bmsg[i * WANT : i * WANT + ENTRIES, :] = col
        bmsg[i * WANT + ENTRIES : (i + 1) * WANT, :] = mine
    idrow[...] = row.astype(F32)


def adjoint_terms(blocks, u_rows, msg, extra, zmsg):
    for r in range(RB):
        spread = jnp.transpose(jnp.broadcast_to(u_rows[r], (BS, BS)))
        for k in range(NNZ):
            e = r * NNZ + k
            msg[e : e + 1, :] = jnp.sum(blocks[r, k] * spread, axis=0, keepdims=True)
    msg[ENTRIES : ENTRIES + 1, :] = extra
    whole = msg[0:ZCH, :]
    for z in range(Z):
        zmsg[z * ZCH : (z + 1) * ZCH, :] = whole


def forward_rows(blocks, chosen, acc):
    for r in range(RB):
        total = blocks[r, 0] * chosen[r * NNZ : r * NNZ + 1, :]
        for k in range(1, NNZ):
            e = r * NNZ + k
            total = total + blocks[r, k] * chosen[e : e + 1, :]
        acc[r * BS : (r + 1) * BS, :] = total
    sums = lax.dot_general(
        jnp.ones((8, BS), F32),
        acc[...],
        (((1,), (1,)), ((), ())),
        precision=lax.Precision.HIGHEST,
        preferred_element_type=F32,
    )
    return [sums[0:1, r * BS : (r + 1) * BS] for r in range(RB)]


def first_kernel(blocks, seis, signs, idrow, data, zmsg, msg):
    signed = (2 * signs[...] - 1).astype(F32) * seis[...]
    whole = jnp.sum(signed, axis=0, keepdims=True)
    rows = [whole[:, r * BS : (r + 1) * BS] for r in range(RB)]
    for r in range(RB):
        data[r : r + 1, :] = rows[r]
    square = jnp.sum(whole * whole, axis=1, keepdims=True)
    ids = idrow[0:1, :]
    adjoint_terms(blocks, rows, msg, jnp.where(ids < 0.0, square, ids), zmsg)


def select_sum(arrived, ids, wanted, pmsg, extra):
    terms = jnp.concatenate([arrived[z * ZCH : z * ZCH + ENTRIES, :] for z in range(Z)], axis=0)
    high = terms.astype(BF16)
    rest = terms - high.astype(F32)
    mid = rest.astype(BF16)
    low = (rest - mid.astype(F32)).astype(BF16)
    pick = jnp.concatenate(
        [jnp.where(wanted[...] == ids[t : t + 1, :], 1.0, 0.0).astype(BF16) for t in range(Z * ENTRIES // BS)], axis=1
    )
    sums = jnp.dot(pick, low, preferred_element_type=F32)
    sums = sums + jnp.dot(pick, mid, preferred_element_type=F32)
    sums = sums + jnp.dot(pick, high, preferred_element_type=F32)
    for i in range(N_PLANE):
        pmsg[i * PCH : i * PCH + WANT, :] = sums[i * WANT : (i + 1) * WANT]
        pmsg[i * PCH + WANT : (i + 1) * PCH, :] = extra


def first_select_kernel(arrived, wanted, pmsg, ids):
    lane = lax.broadcasted_iota(jnp.int32, (1, BS), 1)
    extra = jnp.zeros((1, BS), F32)
    for t in range(Z // GROUPS):
        row = jnp.zeros((1, BS), F32)
        for j in range(GROUPS):
            at = (t * GROUPS + j) * ZCH + ENTRIES
            line = arrived[at : at + 1, :]
            row = jnp.where(lane // ENTRIES == j, line, row)
            extra = extra + jnp.where(lane == (j + 1) % GROUPS * ENTRIES, line, 0.0)
        ids[t : t + 1, :] = row
    ids[Z // GROUPS : 8, :] = jnp.zeros((8 - Z // GROUPS, BS), F32)
    select_sum(arrived, ids, wanted, pmsg, jnp.broadcast_to(extra, (8, BS)))


def select_kernel(arrived, wanted, ids, pmsg):
    extra = arrived[ENTRIES : ENTRIES + 1, :]
    for z in range(1, Z):
        extra = extra + arrived[z * ZCH + ENTRIES : z * ZCH + ZCH, :]
    select_sum(arrived, ids, wanted, pmsg, jnp.broadcast_to(extra, (8, BS)))


def plane_sum(arrived):
    total = arrived[0:WANT, :]
    for i in range(1, N_PLANE):
        total = total + arrived[i * PCH : i * PCH + WANT, :]
    return total


def plane_extra(arrived):
    total = arrived[WANT : WANT + 1, :]
    for i in range(1, N_PLANE):
        total = total + arrived[i * PCH + WANT : i * PCH + WANT + 1, :]
    return jnp.sum(total, axis=1, keepdims=True)


def first_forward_kernel(blocks, arrived, data, v_raw, u_one, beta, ymsg, acc):
    beta_one = jnp.sqrt(plane_extra(arrived) + EPS)
    v = plane_sum(arrived) / beta_one
    v_raw[...] = v
    u_one[...] = data[...] / beta_one
    beta[...] = jnp.broadcast_to(beta_one, (8, BS))
    rows = forward_rows(blocks, v, acc)
    own = v[ENTRIES:WANT]
    extra = jnp.sum(own * own, axis=0, keepdims=True)
    for y in range(Y):
        for r in range(RB):
            ymsg[y * 8 + r : y * 8 + r + 1, :] = rows[r]
        ymsg[y * 8 + RB : (y + 1) * 8, :] = jnp.broadcast_to(extra, (8 - RB, BS))


def adjoint_kernel(blocks, arrived, rows_out, zmsg, msg):
    total = arrived[0:8, :]
    for y in range(1, Y):
        total = total + arrived[y * 8 : (y + 1) * 8, :]
    rows_out[...] = total
    adjoint_terms(blocks, [total[r : r + 1, :] for r in range(RB)], msg, total[RB : RB + 1, :], zmsg)


def second_forward_kernel(
    blocks, arrived, v_raw, u_one, rows_one, model_v, model_a, data_u, data_g, alpha, ymsg, acc, msg
):
    alpha_one = jnp.sqrt(plane_extra(arrived) + EPS)
    v = v_raw[...]
    a = plane_sum(arrived) / alpha_one - alpha_one * v
    g = rows_one[0:RB, :] / alpha_one
    data_g[...] = g
    data_u[...] = g - alpha_one * u_one[...]
    alpha[...] = jnp.broadcast_to(alpha_one, (8, BS))
    rows = forward_rows(blocks, a, acc)
    a_own = a[ENTRIES:WANT]
    v_own = v[ENTRIES:WANT] / alpha_one
    model_a[...] = a_own
    model_v[...] = v_own
    for r in range(RB):
        msg[r : r + 1, :] = rows[r]
    for i, pair in enumerate((dot_rows(a_own, a_own), dot_rows(a_own, v_own), dot_rows(v_own, v_own))):
        msg[RB + i : RB + i + 1, :] = pair[0]
        msg[8 + i : 8 + i + 1, :] = pair[1]
    msg[7:8, :] = jnp.zeros((1, BS), F32)
    msg[11:16, :] = jnp.zeros((5, BS), F32)
    whole = msg[...]
    for y in range(Y):
        ymsg[y * 16 : (y + 1) * 16, :] = whole


def products_kernel(arrived, data_u, data_g, data_q, rmsg, high, low):
    q = arrived[0:RB, :]
    for y in range(1, Y):
        q = q + arrived[y * 16 : y * 16 + RB, :]
    data_q[...] = q
    u = data_u[...]
    g = data_g[...]
    pairs = [dot_rows(u, u), dot_rows(q, q), dot_rows(q, g), dot_rows(q, u), dot_rows(g, g), dot_rows(g, u)]
    high[...] = jnp.zeros((16, BS), F32)
    low[...] = jnp.zeros((16, BS), F32)
    for i, pair in enumerate(pairs):
        high[i : i + 1, :] = pair[0]
        low[i : i + 1, :] = pair[1]
    model = (arrived[RB : RB + 3, :], arrived[8:11, :])
    for y in range(1, Y):
        at = y * 16
        model = dd_add(model, (arrived[at + RB : at + RB + 3, :], arrived[at + 8 : at + 11, :]))
    high[6:9, :] = model[0]
    low[6:9, :] = model[1]
    pair = (high[...], low[...])
    step = BS // 2
    while step:
        pair = dd_add(pair, (pltpu.roll(pair[0], step, 1), pltpu.roll(pair[1], step, 1)))
        step //= 2
    lane = lax.broadcasted_iota(jnp.int32, (16, BS), 1)
    sub = lax.broadcasted_iota(jnp.int32, (16, BS), 0)
    line = jnp.where(lane == sub, pair[0], 0.0) + jnp.where(lane == sub + 64, pair[1], 0.0)
    line = jnp.sum(line, axis=0, keepdims=True)
    rmsg[...] = jnp.broadcast_to(line, (N_ROWS, BS))


def last_kernel(arrived, beta, alpha, model_v, model_a, data_u, data_g, data_q, model, data_dir):
    total = arrived[...]
    pair = fold_rows((total, jnp.zeros_like(total)))
    lane = lax.broadcasted_iota(jnp.int32, (1, BS), 1)

    def take(line, i):
        return jnp.sum(jnp.where(lane == i, line, 0.0), axis=1, keepdims=True)

    def dot(i):
        low = take(pair[1], i) + (take(pair[0], 64 + i) + take(pair[1], 64 + i))
        return dd_add((take(pair[0], i), jnp.zeros((1, 1), F32)), (low, jnp.zeros((1, 1), F32)))

    uu, qq, qg, qu, gg, gu, aa, av, vv = [dot(i) for i in range(DOTS)]
    beta_one = beta[0:1, 0:1]
    alpha_one = alpha[0:1, 0:1]
    beta_two = jnp.sqrt(uu[0] + EPS)
    b_sq = two_prod(beta_two, beta_two)
    square = dd_add(dd_mul(b_sq, dd_add(dd_mul(b_sq, vv), dd_scale(av, -2.0))), aa)
    square = jnp.maximum(square[0] / b_sq[0], 0.0)
    alpha_two = jnp.sqrt(square + EPS)
    a_sq = two_prod(alpha_two, alpha_two)
    part = dd_add(dd_mul(b_sq, dd_add(dd_mul(b_sq, gg), dd_scale(qg, -2.0))), qq)
    part = dd_add(part, dd_mul(a_sq, dd_add(dd_mul(a_sq, uu), dd_scale(qu, -2.0))))
    part = dd_add(part, dd_scale(dd_mul(dd_mul(a_sq, b_sq), gu), 2.0))
    scale = beta_two * alpha_two
    square = jnp.maximum(part[0], 0.0) / scale / scale
    beta_three = jnp.sqrt(square + EPS)

    rho = jnp.sqrt(alpha_one * alpha_one + beta_two * beta_two)
    cosine = alpha_one / rho
    sine = beta_two / rho
    theta = sine * alpha_two
    rhobar = -cosine * alpha_two
    phi = cosine * beta_one
    phibar = sine * beta_one
    v_one = model_v[...]
    v_two = (model_a[...] / beta_two - beta_two * v_one) / alpha_two
    found = phi / rho * v_one
    w = v_two - theta / rho * v_one
    rho = jnp.sqrt(rhobar * rhobar + beta_three * beta_three)
    phi = rhobar / rho * phibar
    model[...] = found + phi / rho * w
    u_three = (data_q[...] - b_sq[0] * data_g[...] - a_sq[0] * data_u[...]) / scale
    data_dir[...] = u_three / beta_three


def exchange(array, axes, peers):
    n = array.shape[0] // peers
    if n % 8 == 0:
        return lax.all_to_all(array.reshape(peers, n, BS), axes, 0, 0, tiled=True).reshape(array.shape)
    return lax.all_to_all(array.reshape(peers * n, 1, BS), axes, 0, 0, tiled=True).reshape(array.shape)


def last_adjoint(blocks, slot, u_vec, v_vec):
    terms = jnp.einsum("rkij,ri->rkj", blocks, u_vec, precision=lax.Precision.HIGHEST)
    targets = lax.broadcasted_iota(jnp.int32, (OWN * N_ROWS, 1), 0)
    pick = (targets == slot[None, :]).astype(F32)
    total = jnp.dot(pick, terms.reshape(ENTRIES, BS), precision=lax.Precision.HIGHEST)
    v_vec = lax.psum_scatter(total, ROWS, scatter_dimension=0, tiled=True) - v_vec
    return v_vec, jnp.sqrt(lax.psum(jnp.sum(v_vec * v_vec), ROWS + ("y",)) + EPS)


def on_device(frechet, pattern, ownership, seismograms, signs):
    blocks = frechet[0]
    place = lax.axis_index(ROWS).astype(jnp.int32)
    group = lax.axis_index("z").astype(jnp.int32) % GROUPS
    me = jnp.stack([place, group])
    size = blocks.size
    msg = pltpu.VMEM((ENTRIES + 8, BS), F32)
    acc = pltpu.VMEM((RB * BS, BS), F32)
    row4, row8 = (RB, BS), (8, BS)
    zshape, pshape = (Z * ZCH, BS), (N_PLANE * PCH, BS)
    heavy = dict(flops=2 * size, moved=4 * size)

    bmsg, idrow = call(ids_kernel, [(N_PLANE * WANT, BS), row8], [SMEM] * 3)(pattern.reshape(-1), ownership, me)
    wanted = exchange(bmsg, PLANE, N_PLANE)

    data, zmsg = call(first_kernel, [row4, zshape], [VMEM] * 4, [msg], **heavy)(blocks, seismograms, signs, idrow)
    pmsg, ids = call(first_select_kernel, [pshape, row8], [VMEM] * 2)(exchange(zmsg, "z", Z), wanted)
    v_raw, u_one, beta, ymsg = call(
        first_forward_kernel, [(WANT, BS), row4, row8, (Y * 8, BS)], [VMEM] * 3, [acc], **heavy
    )(blocks, exchange(pmsg, PLANE, N_PLANE), data)
    rows_one, zmsg = call(adjoint_kernel, [row8, zshape], [VMEM] * 2, [msg], **heavy)(blocks, exchange(ymsg, "y", Y))
    (pmsg,) = call(select_kernel, [pshape], [VMEM] * 3)(exchange(zmsg, "z", Z), wanted, ids)
    model_v, model_a, data_u, data_g, alpha, ymsg = call(
        second_forward_kernel,
        [(OWN, BS), (OWN, BS), row4, row4, row8, (Y * 16, BS)],
        [VMEM] * 5,
        [acc, pltpu.VMEM((16, BS), F32)],
        **heavy,
    )(blocks, exchange(pmsg, PLANE, N_PLANE), v_raw, u_one, rows_one)
    data_q, rmsg = call(
        products_kernel, [row4, (N_ROWS, BS)], [VMEM] * 3, [pltpu.VMEM((16, BS), F32)] * 2
    )(exchange(ymsg, "y", Y), data_u, data_g)
    model, data_dir = call(last_kernel, [(OWN, BS), row4], [VMEM] * 8)(
        exchange(rmsg, ROWS, N_ROWS), beta, alpha, model_v, model_a, data_u, data_g, data_q
    )
    last_adjoint(blocks, ownership[pattern.reshape(-1)], data_dir, model_v)
    return model.reshape(1, OWN * BS), data_dir.reshape(-1)


def solution(mesh):
    split = Mesh(mesh.devices.reshape(X, Z, CORE, Y), ("x", "z", "core", "y"))
    placed = (P("y", ROWS), P(ROWS), P(), P(None, ROWS), P(None, ROWS))
    return jax.shard_map(
        on_device,
        mesh=split,
        in_specs=placed,
        out_specs=(P("y", ROWS), P(ROWS)),
        check_vma=False,
    )
```

time: 1770 us -> 136 us (0.08)
  blocking collectives: 996 us -> 112 us
  waiting for transfers between devices: 732 us -> 2.65 us
    psum x7 -> x0, blocking collectives: 996 us -> none  [the longest x3 753 us: data_norm(): return jnp.sqrt(lax.psum(jnp.sum(values * values), 'rows') + EPS)]
    reduce_scatter x2 -> x0, waiting for transfers between devices: 480 us -> none  [adjoint(): lax.psum_scatter(jnp.dot(select, terms, precision=lax.Precision.HIGHEST),...]
    all_gather x2 -> x0, waiting for transfers between devices: 252 us -> none  [on_device(): lax.all_gather(v_vec.reshape(owned_blocks, width), 'rows', axis=0, tiled=...]
    all_to_all x0 -> x7, blocking collectives: none -> 112 us  [the longest x3 65.5 us: exchange(): lax.all_to_all(array.reshape(peers * n, 1, BS), axes, 0, 0, tiled=True)]
  transfers between devices with their start and end apart: 4 -> 1, of which waited for: 4 -> 1; matrix products, arithmetic and copies ran while one was open for 0% -> 0% of each run, Pallas kernels for 0% -> 0%
where the time goes in v1:
time: 136 us; the launch traced here: 135 us
  blocking collectives  112 us (82%)
  starting transfers between devices  10.2 us (7%)
  Pallas kernels  5.52 us (4%)
  local copies, waits for them, and re-layouts  4.45 us (3%)
  waiting for transfers between devices  2.65 us (2%)
    all_to_all x3, blocking collectives, exchange(): lax.all_to_all(array.reshape(peers * n, 1, BS), axes, 0, 0, tiled=True)  65.5 us
    all_to_all x4, blocking collectives, exchange(): lax.all_to_all(array.reshape(peers, n, BS), axes, 0, 0, tiled=True)  46.1 us
    all_to_all x1, starting transfers between devices, exchange(): lax.all_to_all(array.reshape(peers, n, BS), axes, 0, 0, tiled=True)  10.2 us
    unnamed x10, local copies, waits for them, and re-layouts  3.68 us
  transfers between devices with their start and end apart: 1, of which 1 were waited for; matrix products, arithmetic and copies ran while one was open for 0% of the time, Pallas kernels for 0%

profile of v1, /device:TPU:1, one launch (start us, length us, event | category | flops | bytes accessed | tf_op | source)
XLA Modules:
  0.0 135.2 jit_solution(13680490961580668456)
XLA Ops:
  0.6 0.8 reshape.61.pat
  1.4 0.1 pad_add_fusion.me
  1.5 0.0 copy-start.4
  1.5 0.7 copy-done.4
  2.2 1.4 %shard_map.68 = (f32[384,128]{1,0:T(8,128)}, f32[8,128]{1,0:T(8,128)S(1)}) custom-call(s32[32]{0:T(128)S(1)} %reshape.61.pat, s32[2048]{0:T(1024)S(1)} %copy-done.4, s32[2]{0:T(128)S(1)} %pad_add_fusion.me), custom_call_target="tpu_custom_call" | custom-call | tf_op jit(solution)/shard_map/pallas_call | solution.py:361
  3.6 10.2 %all-to-all-start.1 = ((f32[8,48,128]{2,1,0:T(8,128)}), f32[8,48,128]{2,1,0:T(8,128)S(1)}, u32[]{:S(2)}, u32[]{:S(2)}) async-start(f32[8,48,128]{2,1,0:T(8,128)} %bitcast.6), calls=%async_computation.1 | async-start | bytes 393216 | tf_op jit(solution)/shard_map/all_to_all | solution.py:336
  13.7 0.0 copy-start
  13.8 1.6 %copy-done = f32[1,4,8,128,128]{4,3,2,1,0:T(8,128)S(1)} copy-done((f32[1,4,8,128,128]{4,3,2,1,0:T(8,128)S(1)}, f32[1,4,8,128,128]{4,3,2,1,0:T(8,128)}, u32[]{:S(2)}) %copy-start) | copy-done | bytes 2097176
  15.3 0.0 copy-start.2
  15.3 0.7 copy-done.2
  16.0 0.0 copy-start.3
  16.0 0.7 copy-done.3
  16.7 0.0 copy-start.1
  16.7 0.3 shard_map.69
  17.0 2.7 %all-to-all-done.1 = f32[8,48,128]{2,1,0:T(8,128)S(1)} async-done(((f32[8,48,128]{2,1,0:T(8,128)}), f32[8,48,128]{2,1,0:T(8,128)S(1)}, u32[]{:S(2)}, u32[]{:S(2)}) %all-to-all-start.1) | async-done | bytes 196640 | tf_op jit(solution)/shard_map/all_to_all | solution.py:336
  19.7 23.4 %all_to_all.40 = f32[528,1,128]{2,1,0:T(1,128)S(1)} all-to-all(f32[528,1,128]{2,1,0:T(1,128)S(1)} %bitcast.38), channel_id=1, replica_groups=mesh['x'=4,'z'=16,'core'=2,'y'=4] {'z'}, dimensions={0} | all-to-all | bytes 540672 | tf_op jit(solution)/shard_map/all_to_all | solution.py:337
  43.0 0.5 shard_map.70
  43.5 15.4 %all_to_all.41 = f32[8,56,128]{2,1,0:T(8,128)S(1)} all-to-all(f32[8,56,128]{2,1,0:T(8,128)S(1)} %bitcast.41), channel_id=1, replica_groups=mesh['x'=4,'z'=16,'core'=2,'y'=4] {'x','core'}, dimensions={0} | all-to-all | bytes 458752 | tf_op jit(solution)/shard_map/all_to_all | solution.py:336
  58.9 0.0 copy-done.1
  58.9 0.5 shard_map.71
  59.4 8.2 %all_to_all.42 = f32[4,8,128]{2,1,0:T(8,128)S(1)} all-to-all(f32[4,8,128]{2,1,0:T(8,128)S(1)} %bitcast.46), channel_id=1, replica_groups=mesh['x'=4,'z'=16,'core'=2,'y'=4] {'y'}, dimensions={0} | all-to-all | bytes 32768 | tf_op jit(solution)/shard_map/all_to_all | solution.py:336
  67.6 0.3 shard_map.72
  67.9 18.0 %all_to_all.43 = f32[528,1,128]{2,1,0:T(1,128)S(1)} all-to-all(f32[528,1,128]{2,1,0:T(1,128)S(1)} %bitcast.39), channel_id=1, replica_groups=mesh['x'=4,'z'=16,'core'=2,'y'=4] {'z'}, dimensions={0} | all-to-all | bytes 540672 | tf_op jit(solution)/shard_map/all_to_all | solution.py:337
  85.9 0.5 shard_map.73
  86.4 15.9 %all_to_all.44 = f32[8,56,128]{2,1,0:T(8,128)S(1)} all-to-all(f32[8,56,128]{2,1,0:T(8,128)S(1)} %bitcast.37), channel_id=1, replica_groups=mesh['x'=4,'z'=16,'core'=2,'y'=4] {'x','core'}, dimensions={0} | all-to-all | bytes 458752 | tf_op jit(solution)/shard_map/all_to_all | solution.py:336
  102.3 0.6 shard_map.74
  102.9 6.7 %all_to_all.45 = f32[4,16,128]{2,1,0:T(8,128)S(1)} all-to-all(f32[4,16,128]{2,1,0:T(8,128)S(1)} %bitcast.45), channel_id=1, replica_groups=mesh['x'=4,'z'=16,'core'=2,'y'=4] {'y'}, dimensions={0} | all-to-all | bytes 65536 | tf_op jit(solution)/shard_map/all_to_all | solution.py:336
  109.5 0.6 shard_map.75
  110.1 24.1 %all_to_all.46 = f32[128,1,128]{2,1,0:T(1,128)S(1)} all-to-all(f32[128,1,128]{2,1,0:T(1,128)S(1)} %bitcast.44), channel_id=1, replica_groups=mesh['x'=4,'z'=16,'core'=2,'y'=4] {'x','z','core'}, dimensions={0} | all-to-all | bytes 131072 | tf_op jit(solution)/shard_map/all_to_all | solution.py:337
  134.2 0.9 shard_map.76
Async XLA Ops:
  1.5 0.7 copy-start.4
  3.6 16.1 %all-to-all-start.1 = ((f32[8,48,128]{2,1,0:T(8,128)}), f32[8,48,128]{2,1,0:T(8,128)S(1)}, u32[]{:S(2)}, u32[]{:S(2)}) async-start(f32[8,48,128]{2,1,0:T(8,128)} %bitcast.6), calls=%async_computation.1 | async-start | bytes 393216 | tf_op jit(solution)/shard_map/all_to_all | solution.py:336
  13.7 1.6 %copy-start = (f32[1,4,8,128,128]{4,3,2,1,0:T(8,128)S(1)}, f32[1,4,8,128,128]{4,3,2,1,0:T(8,128)}, u32[]{:S(2)}) copy-start(f32[1,4,8,128,128]{4,3,2,1,0:T(8,128)} %param.5) | copy-start | bytes 6291460
  15.3 0.7 copy-start.2
  16.0 0.7 copy-start.3
  16.7 42.2 %copy-start.1 = (f32[1,4,8,128,128]{4,3,2,1,0:T(8,128)S(1)}, f32[1,4,8,128,128]{4,3,2,1,0:T(8,128)}, u32[]{:S(2)}) copy-start(f32[1,4,8,128,128]{4,3,2,1,0:T(8,128)} %param.5) | copy-start | bytes 6291460

commit v2 on v1

--- a/solution.py
+++ b/solution.py
@@ -24,6 +24,7 @@
 WANT = ENTRIES + OWN
 ZCH = ENTRIES + 1
 PCH = WANT + 8
+PRODUCTS = 12
 GROUPS = BS // ENTRIES
 DOTS = 9
 
@@ -88,6 +89,13 @@
     return pair
 
 
+def pick_row(a, i):
+    row = a[0:1, :]
+    for r in range(1, a.shape[0]):
+        row = jnp.where(i == r, a[r : r + 1, :], row)
+    return row
+
+
 def dot_rows(a, b):
     return fold_rows(two_prod(a, b))
 
@@ -98,7 +106,7 @@
     col = jnp.zeros((ENTRIES, BS), jnp.int32)
     row = jnp.full((8, BS), -1, jnp.int32)
     for e in range(ENTRIES):
-        s = own[pat[e]]
+        s = own[pat[e // NNZ, e % NNZ]]
         col = jnp.where(sub == e, s, col)
         row = jnp.where(lane == e, s, row)
     mine = me[0] * OWN + lax.broadcasted_iota(jnp.int32, (OWN, BS), 0)
@@ -156,8 +164,9 @@
     rest = terms - high.astype(F32)
     mid = rest.astype(BF16)
     low = (rest - mid.astype(F32)).astype(BF16)
+    names = wanted[...]
     pick = jnp.concatenate(
-        [jnp.where(wanted[...] == ids[t : t + 1, :], 1.0, 0.0).astype(BF16) for t in range(Z * ENTRIES // BS)], axis=1
+        [jnp.where(names == ids[t : t + 1, :], 1.0, 0.0).astype(BF16) for t in range(Z * ENTRIES // BS)], axis=1
     )
     sums = jnp.dot(pick, low, preferred_element_type=F32)
     sums = sums + jnp.dot(pick, mid, preferred_element_type=F32)
@@ -227,14 +236,15 @@
 
 
 def second_forward_kernel(
-    blocks, arrived, v_raw, u_one, rows_one, model_v, model_a, data_u, data_g, alpha, ymsg, acc, msg
+    blocks, arrived, v_raw, u_one, rows_one, me, model_v, model_a, data_u, data_g, alpha, ymsg, acc, msg
 ):
     alpha_one = jnp.sqrt(plane_extra(arrived) + EPS)
     v = v_raw[...]
     a = plane_sum(arrived) / alpha_one - alpha_one * v
     g = rows_one[0:RB, :] / alpha_one
     data_g[...] = g
-    data_u[...] = g - alpha_one * u_one[...]
+    u = g - alpha_one * u_one[...]
+    data_u[...] = u
     alpha[...] = jnp.broadcast_to(alpha_one, (8, BS))
     rows = forward_rows(blocks, a, acc)
     a_own = a[ENTRIES:WANT]
@@ -243,35 +253,46 @@
     model_v[...] = v_own
     for r in range(RB):
         msg[r : r + 1, :] = rows[r]
+    y = me[2]
+    msg[RB : RB + 1, :] = pick_row(g, y)
+    msg[RB + 1 : RB + 2, :] = pick_row(u, y)
     for i, pair in enumerate((dot_rows(a_own, a_own), dot_rows(a_own, v_own), dot_rows(v_own, v_own))):
-        msg[RB + i : RB + i + 1, :] = pair[0]
-        msg[8 + i : 8 + i + 1, :] = pair[1]
-    msg[7:8, :] = jnp.zeros((1, BS), F32)
-    msg[11:16, :] = jnp.zeros((5, BS), F32)
-    whole = msg[...]
-    for y in range(Y):
-        ymsg[y * 16 : (y + 1) * 16, :] = whole
-
-
-def products_kernel(arrived, data_u, data_g, data_q, rmsg, high, low):
-    q = arrived[0:RB, :]
-    for y in range(1, Y):
-        q = q + arrived[y * 16 : y * 16 + RB, :]
-    data_q[...] = q
-    u = data_u[...]
-    g = data_g[...]
+        msg[RB + 2 + i : RB + 3 + i, :] = pair[0]
+        msg[RB + 5 + i : RB + 6 + i, :] = pair[1]
+    whole = msg[0:PRODUCTS, :]
+    for i in range(N_PLANE * Y):
+        ymsg[i * PRODUCTS : (i + 1) * PRODUCTS, :] = whole
+
+
+def products_kernel(arrived, me, data_q, rmsg, q_all, g_all, u_all, high, low):
+    mine = jnp.zeros((RB, BS), F32)
+    model = []
+    for i in range(N_PLANE):
+        at = i * Y * PRODUCTS
+        q = arrived[at : at + RB, :]
+        for y in range(1, Y):
+            q = q + arrived[at + y * PRODUCTS : at + y * PRODUCTS + RB, :]
+        mine = jnp.where(me[3] == i, q, mine)
+        q_all[i * RB : (i + 1) * RB, :] = q
+        for y in range(Y):
+            source = at + y * PRODUCTS + RB
+            g_all[i * RB + y : i * RB + y + 1, :] = arrived[source : source + 1, :]
+            u_all[i * RB + y : i * RB + y + 1, :] = arrived[source + 1 : source + 2, :]
+            model.append((arrived[source + 2 : source + 5, :], arrived[source + 5 : source + 8, :]))
+    data_q[...] = mine
+    q = q_all[...]
+    u = u_all[...]
+    g = g_all[...]
     pairs = [dot_rows(u, u), dot_rows(q, q), dot_rows(q, g), dot_rows(q, u), dot_rows(g, g), dot_rows(g, u)]
     high[...] = jnp.zeros((16, BS), F32)
     low[...] = jnp.zeros((16, BS), F32)
     for i, pair in enumerate(pairs):
         high[i : i + 1, :] = pair[0]
         low[i : i + 1, :] = pair[1]
-    model = (arrived[RB : RB + 3, :], arrived[8:11, :])
-    for y in range(1, Y):
-        at = y * 16
-        model = dd_add(model, (arrived[at + RB : at + RB + 3, :], arrived[at + 8 : at + 11, :]))
-    high[6:9, :] = model[0]
-    low[6:9, :] = model[1]
+    while len(model) > 1:
+        model = [dd_add(model[i], model[i + 1]) for i in range(0, len(model), 2)]
+    high[6:9, :] = model[0][0]
+    low[6:9, :] = model[0][1]
     pair = (high[...], low[...])
     step = BS // 2
     while step:
@@ -281,7 +302,7 @@
     sub = lax.broadcasted_iota(jnp.int32, (16, BS), 0)
     line = jnp.where(lane == sub, pair[0], 0.0) + jnp.where(lane == sub + 64, pair[1], 0.0)
     line = jnp.sum(line, axis=0, keepdims=True)
-    rmsg[...] = jnp.broadcast_to(line, (N_ROWS, BS))
+    rmsg[...] = jnp.broadcast_to(line, (Z, BS))
 
 
 def last_kernel(arrived, beta, alpha, model_v, model_a, data_u, data_g, data_q, model, data_dir):
@@ -350,7 +371,8 @@
     blocks = frechet[0]
     place = lax.axis_index(ROWS).astype(jnp.int32)
     group = lax.axis_index("z").astype(jnp.int32) % GROUPS
-    me = jnp.stack([place, group])
+    plane = lax.axis_index(PLANE).astype(jnp.int32)
+    me = jnp.stack([place, group, lax.axis_index("y").astype(jnp.int32), plane])
     size = blocks.size
     msg = pltpu.VMEM((ENTRIES + 8, BS), F32)
     acc = pltpu.VMEM((RB * BS, BS), F32)
@@ -358,7 +380,7 @@
     zshape, pshape = (Z * ZCH, BS), (N_PLANE * PCH, BS)
     heavy = dict(flops=2 * size, moved=4 * size)
 
-    bmsg, idrow = call(ids_kernel, [(N_PLANE * WANT, BS), row8], [SMEM] * 3)(pattern.reshape(-1), ownership, me)
+    bmsg, idrow = call(ids_kernel, [(N_PLANE * WANT, BS), row8], [SMEM] * 3)(pattern, ownership, me)
     wanted = exchange(bmsg, PLANE, N_PLANE)
 
     data, zmsg = call(first_kernel, [row4, zshape], [VMEM] * 4, [msg], **heavy)(blocks, seismograms, signs, idrow)
@@ -370,16 +392,19 @@
     (pmsg,) = call(select_kernel, [pshape], [VMEM] * 3)(exchange(zmsg, "z", Z), wanted, ids)
     model_v, model_a, data_u, data_g, alpha, ymsg = call(
         second_forward_kernel,
-        [(OWN, BS), (OWN, BS), row4, row4, row8, (Y * 16, BS)],
-        [VMEM] * 5,
+        [(OWN, BS), (OWN, BS), row4, row4, row8, (N_PLANE * Y * PRODUCTS, BS)],
+        [VMEM] * 5 + [SMEM],
         [acc, pltpu.VMEM((16, BS), F32)],
         **heavy,
-    )(blocks, exchange(pmsg, PLANE, N_PLANE), v_raw, u_one, rows_one)
+    )(blocks, exchange(pmsg, PLANE, N_PLANE), v_raw, u_one, rows_one, me)
     data_q, rmsg = call(
-        products_kernel, [row4, (N_ROWS, BS)], [VMEM] * 3, [pltpu.VMEM((16, BS), F32)] * 2
-    )(exchange(ymsg, "y", Y), data_u, data_g)
+        products_kernel,
+        [row4, (Z, BS)],
+        [VMEM, SMEM],
+        [pltpu.VMEM((N_PLANE * RB, BS), F32)] * 3 + [pltpu.VMEM((16, BS), F32)] * 2,
+    )(exchange(ymsg, PLANE + ("y",), N_PLANE * Y), me)
     model, data_dir = call(last_kernel, [(OWN, BS), row4], [VMEM] * 8)(
-        exchange(rmsg, ROWS, N_ROWS), beta, alpha, model_v, model_a, data_u, data_g, data_q
+        exchange(rmsg, "z", Z), beta, alpha, model_v, model_a, data_u, data_g, data_q
     )
     last_adjoint(blocks, ownership[pattern.reshape(-1)], data_dir, model_v)
     return model.reshape(1, OWN * BS), data_dir.reshape(-1)

time: 136 us -> 134 us (0.985)
  blocking collectives: 112 us -> 109 us
    all_to_all x4 -> x3, blocking collectives: 46.1 us -> 39.5 us  [exchange(): lax.all_to_all(array.reshape(peers, n, BS), axes, 0, 0, tiled=True)]
    all_to_all x3 -> x4, blocking collectives: 65.5 us -> 69.7 us  [exchange(): lax.all_to_all(array.reshape(peers * n, 1, BS), axes, 0, 0, tiled=True)]
    unnamed x10 -> x12, local copies, waits for them, and re-layouts: 3.68 us -> 4.37 us
where the time goes in v2:
time: 134 us
  blocking collectives  109 us (81%)
  starting transfers between devices  10.2 us (8%)
  Pallas kernels  6.77 us (5%)
  local copies, waits for them, and re-layouts  4.37 us (3%)
  waiting for transfers between devices  2.65 us (2%)
    all_to_all x4, blocking collectives, exchange(): lax.all_to_all(array.reshape(peers * n, 1, BS), axes, 0, 0, tiled=True)  69.7 us
    all_to_all x3, blocking collectives, exchange(): lax.all_to_all(array.reshape(peers, n, BS), axes, 0, 0, tiled=True)  39.5 us
    all_to_all x1, starting transfers between devices, exchange(): lax.all_to_all(array.reshape(peers, n, BS), axes, 0, 0, tiled=True)  10.2 us
    unnamed x12, local copies, waits for them, and re-layouts  4.37 us
  transfers between devices with their start and end apart: 1, of which 1 were waited for; matrix products, arithmetic and copies ran while one was open for 0% of the time, Pallas kernels for 0%

profile of v2, /device:TPU:1, one launch (start us, length us, event | category | flops | bytes accessed | tf_op | source)
XLA Modules:
  0.0 133.9 jit_solution(5411865458077318285)
XLA Ops:
  0.6 0.1 pad_add_fusion.me
  0.7 0.0 copy-start.4
  0.7 0.7 copy-done.4
  1.4 0.0 copy-start.5
  1.4 0.7 copy-done.5
  2.1 1.4 %shard_map.68 = (f32[384,128]{1,0:T(8,128)}, f32[8,128]{1,0:T(8,128)S(1)}) custom-call(s32[4,8]{1,0:T(4,128)S(1)} %copy-done.5, s32[2048]{0:T(1024)S(1)} %copy-done.4, s32[4]{0:T(128)S(1)} %pad_add_fusion.me), custom_call_target="tpu_custom_call" | custom-call | tf_op jit(solution)/shard_map/pallas_call | solution.py:383
  3.5 10.2 %all-to-all-start.1 = ((f32[8,48,128]{2,1,0:T(8,128)}), f32[8,48,128]{2,1,0:T(8,128)S(1)}, u32[]{:S(2)}, u32[]{:S(2)}) async-start(f32[8,48,128]{2,1,0:T(8,128)} %bitcast.8), calls=%async_computation.1 | async-start | bytes 393216 | tf_op jit(solution)/shard_map/all_to_all | solution.py:357
  13.7 0.0 copy-start
  13.7 1.6 %copy-done = f32[1,4,8,128,128]{4,3,2,1,0:T(8,128)S(1)} copy-done((f32[1,4,8,128,128]{4,3,2,1,0:T(8,128)S(1)}, f32[1,4,8,128,128]{4,3,2,1,0:T(8,128)}, u32[]{:S(2)}) %copy-start) | copy-done | bytes 2097176
  15.3 0.0 copy-start.2
  15.3 0.7 copy-done.2
  16.0 0.0 copy-start.3
  16.0 0.7 copy-done.3
  16.7 0.0 copy-start.1
  16.7 0.3 shard_map.69
  17.0 2.7 %all-to-all-done.1 = f32[8,48,128]{2,1,0:T(8,128)S(1)} async-done(((f32[8,48,128]{2,1,0:T(8,128)}), f32[8,48,128]{2,1,0:T(8,128)S(1)}, u32[]{:S(2)}, u32[]{:S(2)}) %all-to-all-start.1) | async-done | bytes 196640 | tf_op jit(solution)/shard_map/all_to_all | solution.py:357
  19.6 23.4 %all_to_all.40 = f32[528,1,128]{2,1,0:T(1,128)S(1)} all-to-all(f32[528,1,128]{2,1,0:T(1,128)S(1)} %bitcast.43), channel_id=1, replica_groups=mesh['x'=4,'z'=16,'core'=2,'y'=4] {'z'}, dimensions={0} | all-to-all | bytes 540672 | tf_op jit(solution)/shard_map/all_to_all | solution.py:358
  43.0 0.5 shard_map.70
  43.5 15.4 %all_to_all.41 = f32[8,56,128]{2,1,0:T(8,128)S(1)} all-to-all(f32[8,56,128]{2,1,0:T(8,128)S(1)} %bitcast.45), channel_id=1, replica_groups=mesh['x'=4,'z'=16,'core'=2,'y'=4] {'x','core'}, dimensions={0} | all-to-all | bytes 458752 | tf_op jit(solution)/shard_map/all_to_all | solution.py:357
  58.8 0.0 copy-done.1
  58.8 0.5 shard_map.71
  59.4 8.2 %all_to_all.42 = f32[4,8,128]{2,1,0:T(8,128)S(1)} all-to-all(f32[4,8,128]{2,1,0:T(8,128)S(1)} %bitcast.49), channel_id=1, replica_groups=mesh['x'=4,'z'=16,'core'=2,'y'=4] {'y'}, dimensions={0} | all-to-all | bytes 32768 | tf_op jit(solution)/shard_map/all_to_all | solution.py:357
  67.6 0.3 shard_map.72
  67.8 18.0 %all_to_all.43 = f32[528,1,128]{2,1,0:T(1,128)S(1)} all-to-all(f32[528,1,128]{2,1,0:T(1,128)S(1)} %bitcast.44), channel_id=1, replica_groups=mesh['x'=4,'z'=16,'core'=2,'y'=4] {'z'}, dimensions={0} | all-to-all | bytes 540672 | tf_op jit(solution)/shard_map/all_to_all | solution.py:358
  85.8 0.5 shard_map.73
  86.3 15.9 %all_to_all.44 = f32[8,56,128]{2,1,0:T(8,128)S(1)} all-to-all(f32[8,56,128]{2,1,0:T(8,128)S(1)} %bitcast.41), channel_id=1, replica_groups=mesh['x'=4,'z'=16,'core'=2,'y'=4] {'x','core'}, dimensions={0} | all-to-all | bytes 458752 | tf_op jit(solution)/shard_map/all_to_all | solution.py:357
  102.2 1.1 shard_map.74
  103.4 12.2 %all_to_all.45 = f32[384,1,128]{2,1,0:T(1,128)S(1)} all-to-all(f32[384,1,128]{2,1,0:T(1,128)S(1)} %bitcast.46), channel_id=1, replica_groups=mesh['x'=4,'z'=16,'core'=2,'y'=4] {'x','core','y'}, dimensions={0} | all-to-all | bytes 393216 | tf_op jit(solution)/shard_map/all_to_all | solution.py:358
  115.6 1.3 shard_map.75
  116.8 16.1 %all_to_all.46 = f32[16,1,128]{2,1,0:T(1,128)S(1)} all-to-all(f32[16,1,128]{2,1,0:T(1,128)S(1)} %bitcast.50), channel_id=1, replica_groups=mesh['x'=4,'z'=16,'core'=2,'y'=4] {'z'}, dimensions={0} | all-to-all | bytes 16384 | tf_op jit(solution)/shard_map/all_to_all | solution.py:358
  133.0 0.9 shard_map.76
Async XLA Ops:
  0.7 0.7 copy-start.4
  1.4 0.7 copy-start.5
  3.5 16.1 %all-to-all-start.1 = ((f32[8,48,128]{2,1,0:T(8,128)}), f32[8,48,128]{2,1,0:T(8,128)S(1)}, u32[]{:S(2)}, u32[]{:S(2)}) async-start(f32[8,48,128]{2,1,0:T(8,128)} %bitcast.8), calls=%async_computation.1 | async-start | bytes 393216 | tf_op jit(solution)/shard_map/all_to_all | solution.py:357
  13.7 1.6 %copy-start = (f32[1,4,8,128,128]{4,3,2,1,0:T(8,128)S(1)}, f32[1,4,8,128,128]{4,3,2,1,0:T(8,128)}, u32[]{:S(2)}) copy-start(f32[1,4,8,128,128]{4,3,2,1,0:T(8,128)} %param.5) | copy-start | bytes 6291460
  15.3 0.7 copy-start.2
  16.0 0.7 copy-start.3
  16.7 42.2 %copy-start.1 = (f32[1,4,8,128,128]{4,3,2,1,0:T(8,128)S(1)}, f32[1,4,8,128,128]{4,3,2,1,0:T(8,128)}, u32[]{:S(2)}) copy-start(f32[1,4,8,128,128]{4,3,2,1,0:T(8,128)} %param.5) | copy-start | bytes 6291460

commit v3 on v2

--- a/solution.py
+++ b/solution.py
@@ -30,16 +30,17 @@
 
 VMEM = pl.BlockSpec(memory_space=pltpu.VMEM)
 SMEM = pl.BlockSpec(memory_space=pltpu.SMEM)
-
-
-def call(kernel, outs, ins, scratch=(), flops=0, moved=0):
+HBM = pl.BlockSpec(memory_space=pltpu.HBM)
+
+
+def call(kernel, outs, ins, scratch=(), flops=0, moved=0, vmem=32 * 1024 * 1024):
     return pl.pallas_call(
         kernel,
         out_shape=tuple(jax.ShapeDtypeStruct(s, F32) for s in outs),
         in_specs=list(ins),
         out_specs=tuple(VMEM for _ in outs),
         scratch_shapes=list(scratch),
-        compiler_params=pltpu.CompilerParams(vmem_limit_bytes=32 * 1024 * 1024),
+        compiler_params=pltpu.CompilerParams(vmem_limit_bytes=vmem),
         cost_estimate=pl.CostEstimate(flops=flops, bytes_accessed=moved, transcendentals=0),
     )
 
@@ -100,30 +101,13 @@
     return fold_rows(two_prod(a, b))
 
 
-def ids_kernel(pat, own, me, bmsg, idrow):
-    sub = lax.broadcasted_iota(jnp.int32, (ENTRIES, BS), 0)
-    lane = lax.broadcasted_iota(jnp.int32, (8, BS), 1) - me[1] * ENTRIES
-    col = jnp.zeros((ENTRIES, BS), jnp.int32)
-    row = jnp.full((8, BS), -1, jnp.int32)
-    for e in range(ENTRIES):
-        s = own[pat[e // NNZ, e % NNZ]]
-        col = jnp.where(sub == e, s, col)
-        row = jnp.where(lane == e, s, row)
-    mine = me[0] * OWN + lax.broadcasted_iota(jnp.int32, (OWN, BS), 0)
-    col = col.astype(F32)
-    mine = mine.astype(F32)
-    for i in range(N_PLANE):
-        bmsg[i * WANT : i * WANT + ENTRIES, :] = col
-        bmsg[i * WANT + ENTRIES : (i + 1) * WANT, :] = mine
-    idrow[...] = row.astype(F32)
-
-
-def adjoint_terms(blocks, u_rows, msg, extra, zmsg):
+def adjoint_terms(block, u_rows, msg, extra, zmsg):
     for r in range(RB):
         spread = jnp.transpose(jnp.broadcast_to(u_rows[r], (BS, BS)))
+        row = block(r)
         for k in range(NNZ):
             e = r * NNZ + k
-            msg[e : e + 1, :] = jnp.sum(blocks[r, k] * spread, axis=0, keepdims=True)
+            msg[e : e + 1, :] = jnp.sum(row[k] * spread, axis=0, keepdims=True)
     msg[ENTRIES : ENTRIES + 1, :] = extra
     whole = msg[0:ZCH, :]
     for z in range(Z):
@@ -147,36 +131,74 @@
     return [sums[0:1, r * BS : (r + 1) * BS] for r in range(RB)]
 
 
-def first_kernel(blocks, seis, signs, idrow, data, zmsg, msg):
-    signed = (2 * signs[...] - 1).astype(F32) * seis[...]
+def first_kernel(
+    blocks, seis, signs, pat, own, data, zmsg, named, msg, held, seis_v, signs_v, pat_s, own_s, sems, block_sems
+):
+    small = [
+        pltpu.make_async_copy(src, dst, sems.at[i])
+        for i, (src, dst) in enumerate(((pat, pat_s), (own, own_s), (seis, seis_v), (signs, signs_v)))
+    ]
+    large = [pltpu.make_async_copy(blocks.at[r], held.at[r], block_sems.at[r]) for r in range(RB)]
+    for copy in small + large:
+        copy.start()
+    small[2].wait()
+    small[3].wait()
+    signed = (2 * signs_v[...] - 1).astype(F32) * seis_v[...]
     whole = jnp.sum(signed, axis=0, keepdims=True)
     rows = [whole[:, r * BS : (r + 1) * BS] for r in range(RB)]
     for r in range(RB):
         data[r : r + 1, :] = rows[r]
     square = jnp.sum(whole * whole, axis=1, keepdims=True)
-    ids = idrow[0:1, :]
-    adjoint_terms(blocks, rows, msg, jnp.where(ids < 0.0, square, ids), zmsg)
-
-
-def select_sum(arrived, ids, wanted, pmsg, extra):
+
+    small[0].wait()
+    small[1].wait()
+    sub = lax.broadcasted_iota(jnp.int32, (ENTRIES, BS), 0)
+    lane = lax.broadcasted_iota(jnp.int32, (1, BS), 1) - lax.axis_index("z") % GROUPS * ENTRIES
+    col = jnp.zeros((ENTRIES, BS), jnp.int32)
+    row = jnp.full((1, BS), -1, jnp.int32)
+    for e in range(ENTRIES):
+        s = own_s[pat_s[e // NNZ, e % NNZ]]
+        col = jnp.where(sub == e, s, col)
+        row = jnp.where(lane == e, s, row)
+    named[...] = col.astype(F32)
+    ids = row.astype(F32)
+
+    def block(r):
+        large[r].wait()
+        return [held[r, k] for k in range(NNZ)]
+
+    adjoint_terms(block, rows, msg, jnp.where(ids < 0.0, square, ids), zmsg)
+
+
+def select_sum(arrived, ids, named, pmsg, extra):
     terms = jnp.concatenate([arrived[z * ZCH : z * ZCH + ENTRIES, :] for z in range(Z)], axis=0)
     high = terms.astype(BF16)
     rest = terms - high.astype(F32)
     mid = rest.astype(BF16)
     low = (rest - mid.astype(F32)).astype(BF16)
-    names = wanted[...]
+    step = lax.broadcasted_iota(jnp.int32, (OWN, BS), 0)
+    x_here, z_here, core_here = [lax.axis_index(axis) for axis in ROWS]
+    peers, names = [], []
+    for away in range(X):
+        for other in range(CORE):
+            x, core = (x_here + away) % X, (core_here + other) % CORE
+            peers.append(x * CORE + core)
+            names.append(named[away][other * ENTRIES : (other + 1) * ENTRIES, :])
+            names.append((((x * Z + z_here) * CORE + core) * OWN + step).astype(F32))
+    names = jnp.concatenate(names, axis=0)
     pick = jnp.concatenate(
         [jnp.where(names == ids[t : t + 1, :], 1.0, 0.0).astype(BF16) for t in range(Z * ENTRIES // BS)], axis=1
     )
     sums = jnp.dot(pick, low, preferred_element_type=F32)
     sums = sums + jnp.dot(pick, mid, preferred_element_type=F32)
     sums = sums + jnp.dot(pick, high, preferred_element_type=F32)
-    for i in range(N_PLANE):
-        pmsg[i * PCH : i * PCH + WANT, :] = sums[i * WANT : (i + 1) * WANT]
-        pmsg[i * PCH + WANT : (i + 1) * PCH, :] = extra
-
-
-def first_select_kernel(arrived, wanted, pmsg, ids):
+    for i, peer in enumerate(peers):
+        at = pl.multiple_of(peer * PCH, 8)
+        pmsg[pl.ds(at, WANT), :] = sums[i * WANT : (i + 1) * WANT]
+        pmsg[pl.ds(at + WANT, 8), :] = extra
+
+
+def first_select_kernel(arrived, n0, n1, n2, n3, pmsg, ids):
     lane = lax.broadcasted_iota(jnp.int32, (1, BS), 1)
     extra = jnp.zeros((1, BS), F32)
     for t in range(Z // GROUPS):
@@ -188,14 +210,14 @@
             extra = extra + jnp.where(lane == (j + 1) % GROUPS * ENTRIES, line, 0.0)
         ids[t : t + 1, :] = row
     ids[Z // GROUPS : 8, :] = jnp.zeros((8 - Z // GROUPS, BS), F32)
-    select_sum(arrived, ids, wanted, pmsg, jnp.broadcast_to(extra, (8, BS)))
-
-
-def select_kernel(arrived, wanted, ids, pmsg):
+    select_sum(arrived, ids, (n0, n1, n2, n3), pmsg, jnp.broadcast_to(extra, (8, BS)))
+
+
+def select_kernel(arrived, n0, n1, n2, n3, ids, pmsg):
     extra = arrived[ENTRIES : ENTRIES + 1, :]
     for z in range(1, Z):
         extra = extra + arrived[z * ZCH + ENTRIES : z * ZCH + ZCH, :]
-    select_sum(arrived, ids, wanted, pmsg, jnp.broadcast_to(extra, (8, BS)))
+    select_sum(arrived, ids, (n0, n1, n2, n3), pmsg, jnp.broadcast_to(extra, (8, BS)))
 
 
 def plane_sum(arrived):
@@ -212,11 +234,10 @@
     return jnp.sum(total, axis=1, keepdims=True)
 
 
-def first_forward_kernel(blocks, arrived, data, v_raw, u_one, beta, ymsg, acc):
+def first_forward_kernel(blocks, arrived, v_raw, beta, ymsg, acc):
     beta_one = jnp.sqrt(plane_extra(arrived) + EPS)
     v = plane_sum(arrived) / beta_one
     v_raw[...] = v
-    u_one[...] = data[...] / beta_one
     beta[...] = jnp.broadcast_to(beta_one, (8, BS))
     rows = forward_rows(blocks, v, acc)
     own = v[ENTRIES:WANT]
@@ -232,18 +253,19 @@
     for y in range(1, Y):
         total = total + arrived[y * 8 : (y + 1) * 8, :]
     rows_out[...] = total
-    adjoint_terms(blocks, [total[r : r + 1, :] for r in range(RB)], msg, total[RB : RB + 1, :], zmsg)
+    rows = [total[r : r + 1, :] for r in range(RB)]
+    adjoint_terms(lambda r: [blocks[r, k] for k in range(NNZ)], rows, msg, total[RB : RB + 1, :], zmsg)
 
 
 def second_forward_kernel(
-    blocks, arrived, v_raw, u_one, rows_one, me, model_v, model_a, data_u, data_g, alpha, ymsg, acc, msg
+    blocks, arrived, v_raw, data, beta, rows_one, model_v, model_a, data_u, data_g, alpha, ymsg, acc, msg
 ):
     alpha_one = jnp.sqrt(plane_extra(arrived) + EPS)
     v = v_raw[...]
     a = plane_sum(arrived) / alpha_one - alpha_one * v
     g = rows_one[0:RB, :] / alpha_one
     data_g[...] = g
-    u = g - alpha_one * u_one[...]
+    u = g - alpha_one * (data[...] / beta[0:1, 0:1])
     data_u[...] = u
     alpha[...] = jnp.broadcast_to(alpha_one, (8, BS))
     rows = forward_rows(blocks, a, acc)
@@ -253,18 +275,20 @@
     model_v[...] = v_own
     for r in range(RB):
         msg[r : r + 1, :] = rows[r]
-    y = me[2]
+    y = lax.axis_index("y")
     msg[RB : RB + 1, :] = pick_row(g, y)
     msg[RB + 1 : RB + 2, :] = pick_row(u, y)
     for i, pair in enumerate((dot_rows(a_own, a_own), dot_rows(a_own, v_own), dot_rows(v_own, v_own))):
         msg[RB + 2 + i : RB + 3 + i, :] = pair[0]
         msg[RB + 5 + i : RB + 6 + i, :] = pair[1]
-    whole = msg[0:PRODUCTS, :]
-    for i in range(N_PLANE * Y):
-        ymsg[i * PRODUCTS : (i + 1) * PRODUCTS, :] = whole
-
-
-def products_kernel(arrived, me, data_q, rmsg, q_all, g_all, u_all, high, low):
+    msg[PRODUCTS : 2 * PRODUCTS, :] = msg[0:PRODUCTS, :]
+    whole = msg[...]
+    for i in range(N_PLANE * Y // 2):
+        ymsg[i * 2 * PRODUCTS : (i + 1) * 2 * PRODUCTS, :] = whole
+
+
+def products_kernel(arrived, data_q, rmsg, q_all, g_all, u_all, high, low):
+    here = lax.axis_index("x") * CORE + lax.axis_index("core")
     mine = jnp.zeros((RB, BS), F32)
     model = []
     for i in range(N_PLANE):
@@ -272,7 +296,7 @@
         q = arrived[at : at + RB, :]
         for y in range(1, Y):
             q = q + arrived[at + y * PRODUCTS : at + y * PRODUCTS + RB, :]
-        mine = jnp.where(me[3] == i, q, mine)
+        mine = jnp.where(here == i, q, mine)
         q_all[i * RB : (i + 1) * RB, :] = q
         for y in range(Y):
             source = at + y * PRODUCTS + RB
@@ -369,10 +393,6 @@
 
 def on_device(frechet, pattern, ownership, seismograms, signs):
     blocks = frechet[0]
-    place = lax.axis_index(ROWS).astype(jnp.int32)
-    group = lax.axis_index("z").astype(jnp.int32) % GROUPS
-    plane = lax.axis_index(PLANE).astype(jnp.int32)
-    me = jnp.stack([place, group, lax.axis_index("y").astype(jnp.int32), plane])
     size = blocks.size
     msg = pltpu.VMEM((ENTRIES + 8, BS), F32)
     acc = pltpu.VMEM((RB * BS, BS), F32)
@@ -380,29 +400,45 @@
     zshape, pshape = (Z * ZCH, BS), (N_PLANE * PCH, BS)
     heavy = dict(flops=2 * size, moved=4 * size)
 
-    bmsg, idrow = call(ids_kernel, [(N_PLANE * WANT, BS), row8], [SMEM] * 3)(pattern, ownership, me)
-    wanted = exchange(bmsg, PLANE, N_PLANE)
-
-    data, zmsg = call(first_kernel, [row4, zshape], [VMEM] * 4, [msg], **heavy)(blocks, seismograms, signs, idrow)
-    pmsg, ids = call(first_select_kernel, [pshape, row8], [VMEM] * 2)(exchange(zmsg, "z", Z), wanted)
-    v_raw, u_one, beta, ymsg = call(
-        first_forward_kernel, [(WANT, BS), row4, row8, (Y * 8, BS)], [VMEM] * 3, [acc], **heavy
-    )(blocks, exchange(pmsg, PLANE, N_PLANE), data)
+    data, zmsg, named = call(
+        first_kernel,
+        [row4, zshape, (ENTRIES, BS)],
+        [HBM] * 5,
+        [
+            msg,
+            pltpu.VMEM(blocks.shape, F32),
+            pltpu.VMEM(seismograms.shape, F32),
+            pltpu.VMEM(signs.shape, jnp.int32),
+            pltpu.SMEM(pattern.shape, jnp.int32),
+            pltpu.SMEM(ownership.shape, jnp.int32),
+            pltpu.SemaphoreType.DMA((4,)),
+            pltpu.SemaphoreType.DMA((RB,)),
+        ],
+        vmem=59 * 1024 * 1024,
+        **heavy,
+    )(blocks, seismograms, signs, pattern, ownership)
+    arrived = exchange(zmsg, "z", Z)
+    near = jnp.concatenate([named, lax.ppermute(named, "core", [(0, 1), (1, 0)])], axis=0)
+    named = [near] + [lax.ppermute(near, "x", [((i + d) % X, i) for i in range(X)]) for d in range(1, X)]
+    pmsg, ids = call(first_select_kernel, [pshape, row8], [VMEM] * 5)(arrived, *named)
+    v_raw, beta, ymsg = call(
+        first_forward_kernel, [(WANT, BS), row8, (Y * 8, BS)], [VMEM] * 2, [acc], **heavy
+    )(blocks, exchange(pmsg, PLANE, N_PLANE))
     rows_one, zmsg = call(adjoint_kernel, [row8, zshape], [VMEM] * 2, [msg], **heavy)(blocks, exchange(ymsg, "y", Y))
-    (pmsg,) = call(select_kernel, [pshape], [VMEM] * 3)(exchange(zmsg, "z", Z), wanted, ids)
+    (pmsg,) = call(select_kernel, [pshape], [VMEM] * 6)(exchange(zmsg, "z", Z), *named, ids)
     model_v, model_a, data_u, data_g, alpha, ymsg = call(
         second_forward_kernel,
         [(OWN, BS), (OWN, BS), row4, row4, row8, (N_PLANE * Y * PRODUCTS, BS)],
-        [VMEM] * 5 + [SMEM],
-        [acc, pltpu.VMEM((16, BS), F32)],
+        [VMEM] * 6,
+        [acc, pltpu.VMEM((2 * PRODUCTS, BS), F32)],
         **heavy,
-    )(blocks, exchange(pmsg, PLANE, N_PLANE), v_raw, u_one, rows_one, me)
+    )(blocks, exchange(pmsg, PLANE, N_PLANE), v_raw, data, beta, rows_one)
     data_q, rmsg = call(
         products_kernel,
         [row4, (Z, BS)],
-        [VMEM, SMEM],
+        [VMEM],
         [pltpu.VMEM((N_PLANE * RB, BS), F32)] * 3 + [pltpu.VMEM((16, BS), F32)] * 2,
-    )(exchange(ymsg, PLANE + ("y",), N_PLANE * Y), me)
+    )(exchange(ymsg, PLANE + ("y",), N_PLANE * Y))
     model, data_dir = call(last_kernel, [(OWN, BS), row4], [VMEM] * 8)(
         exchange(rmsg, "z", Z), beta, alpha, model_v, model_a, data_u, data_g, data_q
     )

time: 134 us -> 129 us (0.963)
  blocking collectives: 109 us -> 88.6 us
  starting transfers between devices: 10.2 us -> 29.1 us
  local copies, waits for them, and re-layouts: 4.37 us -> 0.73 us
    all_to_all x4 -> x3, blocking collectives: 69.7 us -> 50.9 us  [exchange(): lax.all_to_all(array.reshape(peers * n, 1, BS), axes, 0, 0, tiled=True)]
    ppermute x0 -> x4, starting transfers between devices: none -> 13.4 us  [the longest x3 10.5 us: on_device(): lax.ppermute(near, 'x', [((i + d) % X, i) for i in range(X)])]
    all_to_all x1, starting transfers between devices: 10.2 us -> 15.8 us  [exchange(): lax.all_to_all(array.reshape(peers * n, 1, BS), axes, 0, 0, tiled=True)]
    unnamed x12 -> x5, local copies, waits for them, and re-layouts: 4.37 us -> 0.73 us
    all_to_all x1, waiting for transfers between devices: 2.65 us -> 0.01 us  [exchange(): lax.all_to_all(array.reshape(peers * n, 1, BS), axes, 0, 0, tiled=True)]
    ppermute x0 -> x4, waiting for transfers between devices: none -> 2.17 us  [the longest x3 1.87 us: on_device(): lax.ppermute(near, 'x', [((i + d) % X, i) for i in range(X)])]
    all_to_all x3, blocking collectives: 39.5 us -> 37.7 us  [exchange(): lax.all_to_all(array.reshape(peers, n, BS), axes, 0, 0, tiled=True)]
    pallas_call x6 -> x5, Pallas kernels: 4.48 us -> 4.95 us  [the longest x1 2.69 us: on_device(): call(first_kernel, [row4, zshape, (ENTRIES, BS)], [HBM] * 5, [msg, pltpu....]
  transfers between devices with their start and end apart: 1 -> 5, of which waited for: 1 -> 2; matrix products, arithmetic and copies ran while one was open for 0% -> 1% of each run, Pallas kernels for 0% -> 0%
where the time goes in v3:
time: 129 us; the launch traced here: 128 us
  blocking collectives  88.6 us (69%)
  starting transfers between devices  29.1 us (23%)
  Pallas kernels  6.7 us (5%)
  waiting for transfers between devices  2.18 us (2%)
    all_to_all x3, blocking collectives, exchange(): lax.all_to_all(array.reshape(peers * n, 1, BS), axes, 0, 0, tiled=True)  50.9 us
    all_to_all x3, blocking collectives, exchange(): lax.all_to_all(array.reshape(peers, n, BS), axes, 0, 0, tiled=True)  37.7 us
    all_to_all x1, starting transfers between devices, exchange(): lax.all_to_all(array.reshape(peers * n, 1, BS), axes, 0, 0, tiled=True)  15.8 us
    ppermute x3, starting transfers between devices, on_device(): lax.ppermute(near, 'x', [((i + d) % X, i) for i in range(X)])  10.5 us
    ppermute x1, starting transfers between devices, on_device(): lax.ppermute(named, 'core', [(0, 1), (1, 0)])  2.86 us
    pallas_call x1, Pallas kernels, on_device(): call(first_kernel, [row4, zshape, (ENTRIES, BS)], [HBM] * 5, [msg, pltpu....  2.69 us
  transfers between devices with their start and end apart: 5, of which 2 were waited for; matrix products, arithmetic and copies ran while one was open for 1% of the time, Pallas kernels for 0%

profile of v3, /device:TPU:1, one launch (start us, length us, event | category | flops | bytes accessed | tf_op | source)
XLA Modules:
  0.0 128.1 jit_solution(14719542006307592690)
XLA Ops:
  0.6 0.0 copy-start
  0.6 2.7 %shard_map.68 = (f32[4,128]{1,0:T(4,128)}, f32[528,128]{1,0:T(8,128)}, f32[32,128]{1,0:T(8,128)}) custom-call(f32[4,8,128,128]{3,2,1,0:T(8,128)} %bitcast.25, f32[4,512]{1,0:T(4,128)} %seis.1, s32[4,512]{1,0:T(4,128)} %signs.1, s32[4,8]{1,0:T(4,128)} %pat.1, s32[2048]{0:T(1024)} %own.1), custom_call_target="tpu_custom_call" | custom-call | flops 1048576 | bytes 2097152 | tf_op jit(solution)/shard_map/pallas_call | solution.py:403
  3.3 15.8 %all-to-all-start = ((f32[528,1,128]{2,1,0:T(1,128)}), f32[528,1,128]{2,1,0:T(1,128)S(1)}, u32[]{:S(2)}, u32[]{:S(2)}) async-start(f32[528,1,128]{2,1,0:T(1,128)} %bitcast.42), calls=%async_computation | async-start | bytes 540672 | tf_op jit(solution)/shard_map/all_to_all | solution.py:382
  19.1 2.9 %collective-permute-start = (f32[32,128]{1,0:T(8,128)}, f32[32,128]{1,0:T(8,128)S(1)}, u32[]{:S(2)}, u32[]{:S(2)}) collective-permute-start(f32[32,128]{1,0:T(8,128)} %get-tuple-element.23), channel_id=1, source_target_pairs={{0,4},{4,0},{1,5},{5,1},{2,6},{6,2},{3,7},{7,3},{8,12},{12,8},{9,1... | collective-permute-start | bytes 49160 | tf_op jit(solution)/shard_map/ppermute | solution.py:421
  22.0 0.7 constant_dynamic-update-slice_fusion.1
  22.7 0.3 collective-permute-done
  23.0 3.1 %collective-permute-start.3 = (f32[64,128]{1,0:T(8,128)S(1)}, f32[64,128]{1,0:T(8,128)S(1)}, u32[]{:S(2)}, u32[]{:S(2)}) collective-permute-start(f32[64,128]{1,0:T(8,128)S(1)} %constant_dynamic-update-slice_fusion.n0), channel_id=1, source_target_pairs={{384,0},{0,128},{128,256},{256,384},{385,1},{1,129},{129,257},{257... | collective-permute-start | bytes 98312 | tf_op jit(solution)/shard_map/ppermute | solution.py:422
  26.1 4.4 %collective-permute-start.2 = (f32[64,128]{1,0:T(8,128)S(1)}, f32[64,128]{1,0:T(8,128)S(1)}, u32[]{:S(2)}, u32[]{:S(2)}) collective-permute-start(f32[64,128]{1,0:T(8,128)S(1)} %constant_dynamic-update-slice_fusion.n0), channel_id=1, source_target_pairs={{256,0},{384,128},{0,256},{128,384},{257,1},{385,129},{1,257},{129... | collective-permute-start | bytes 98312 | tf_op jit(solution)/shard_map/ppermute | solution.py:422
  30.5 3.1 %collective-permute-start.1 = (f32[64,128]{1,0:T(8,128)S(1)}, f32[64,128]{1,0:T(8,128)S(1)}, u32[]{:S(2)}, u32[]{:S(2)}) collective-permute-start(f32[64,128]{1,0:T(8,128)S(1)} %constant_dynamic-update-slice_fusion.n0), channel_id=1, source_target_pairs={{128,0},{256,128},{384,256},{0,384},{129,1},{257,129},{385,257},{1... | collective-permute-start | bytes 98312 | tf_op jit(solution)/shard_map/ppermute | solution.py:422
  33.6 0.0 collective-permute-done.3.n3
  33.6 0.0 collective-permute-done.2.n2
  33.6 1.9 %collective-permute-done.1.n1 = f32[64,128]{1,0:T(8,128)S(1)} collective-permute-done((f32[64,128]{1,0:T(8,128)S(1)}, f32[64,128]{1,0:T(8,128)S(1)}, u32[]{:S(2)}, u32[]{:S(2)}) %collective-permute-start.1) | collective-permute-done | bytes 32800 | tf_op jit(solution)/shard_map/ppermute | solution.py:422
  35.4 0.0 all-to-all-done
  35.4 0.5 shard_map.69
  35.9 13.5 %all_to_all.35 = f32[8,56,128]{2,1,0:T(8,128)S(1)} all-to-all(f32[8,56,128]{2,1,0:T(8,128)S(1)} %bitcast.36), channel_id=1, replica_groups=mesh['x'=4,'z'=16,'core'=2,'y'=4] {'x','core'}, dimensions={0} | all-to-all | bytes 458752 | tf_op jit(solution)/shard_map/all_to_all | solution.py:381
  49.4 0.0 copy-done
  49.4 0.5 shard_map.70
  50.0 0.0 copy-start.1
  50.0 8.3 %all_to_all.36 = f32[4,8,128]{2,1,0:T(8,128)S(1)} all-to-all(f32[4,8,128]{2,1,0:T(8,128)S(1)} %bitcast.40), channel_id=1, replica_groups=mesh['x'=4,'z'=16,'core'=2,'y'=4] {'y'}, dimensions={0} | all-to-all | bytes 32768 | tf_op jit(solution)/shard_map/all_to_all | solution.py:381
  58.3 0.3 shard_map.71
  58.5 22.6 %all_to_all.37 = f32[528,1,128]{2,1,0:T(1,128)S(1)} all-to-all(f32[528,1,128]{2,1,0:T(1,128)S(1)} %bitcast.35), channel_id=1, replica_groups=mesh['x'=4,'z'=16,'core'=2,'y'=4] {'z'}, dimensions={0} | all-to-all | bytes 540672 | tf_op jit(solution)/shard_map/all_to_all | solution.py:382
  81.1 0.5 shard_map.72
  81.6 15.9 %all_to_all.38 = f32[8,56,128]{2,1,0:T(8,128)S(1)} all-to-all(f32[8,56,128]{2,1,0:T(8,128)S(1)} %bitcast.32), channel_id=1, replica_groups=mesh['x'=4,'z'=16,'core'=2,'y'=4] {'x','core'}, dimensions={0} | all-to-all | bytes 458752 | tf_op jit(solution)/shard_map/all_to_all | solution.py:381
  97.5 0.0 copy-done.1
  97.5 0.6 shard_map.73
  98.1 12.2 %all_to_all.39 = f32[384,1,128]{2,1,0:T(1,128)S(1)} all-to-all(f32[384,1,128]{2,1,0:T(1,128)S(1)} %bitcast.37), channel_id=1, replica_groups=mesh['x'=4,'z'=16,'core'=2,'y'=4] {'x','core','y'}, dimensions={0} | all-to-all | bytes 393216 | tf_op jit(solution)/shard_map/all_to_all | solution.py:382
  110.3 0.7 shard_map.74
  111.1 16.1 %all_to_all.40 = f32[16,1,128]{2,1,0:T(1,128)S(1)} all-to-all(f32[16,1,128]{2,1,0:T(1,128)S(1)} %bitcast.41), channel_id=1, replica_groups=mesh['x'=4,'z'=16,'core'=2,'y'=4] {'z'}, dimensions={0} | all-to-all | bytes 16384 | tf_op jit(solution)/shard_map/all_to_all | solution.py:382
  127.2 0.9 shard_map.75
  (1 shorter events, 0.0 us)
Async XLA Ops:
  0.6 48.8 %copy-start = (f32[1,4,8,128,128]{4,3,2,1,0:T(8,128)S(1)}, f32[1,4,8,128,128]{4,3,2,1,0:T(8,128)}, u32[]{:S(2)}) copy-start(f32[1,4,8,128,128]{4,3,2,1,0:T(8,128)} %param.5) | copy-start | bytes 6291460
  3.3 32.1 %all-to-all-start = ((f32[528,1,128]{2,1,0:T(1,128)}), f32[528,1,128]{2,1,0:T(1,128)S(1)}, u32[]{:S(2)}, u32[]{:S(2)}) async-start(f32[528,1,128]{2,1,0:T(1,128)} %bitcast.42), calls=%async_computation | async-start | bytes 540672 | tf_op jit(solution)/shard_map/all_to_all | solution.py:382
  19.1 3.9 %collective-permute-start = (f32[32,128]{1,0:T(8,128)}, f32[32,128]{1,0:T(8,128)S(1)}, u32[]{:S(2)}, u32[]{:S(2)}) collective-permute-start(f32[32,128]{1,0:T(8,128)} %get-tuple-element.23), channel_id=1, source_target_pairs={{0,4},{4,0},{1,5},{5,1},{2,6},{6,2},{3,7},{7,3},{8,12},{12,8},{9,1... | collective-permute-start | bytes 49160 | tf_op jit(solution)/shard_map/ppermute | solution.py:421
  23.0 10.6 %collective-permute-start.3 = (f32[64,128]{1,0:T(8,128)S(1)}, f32[64,128]{1,0:T(8,128)S(1)}, u32[]{:S(2)}, u32[]{:S(2)}) collective-permute-start(f32[64,128]{1,0:T(8,128)S(1)} %constant_dynamic-update-slice_fusion.n0), channel_id=1, source_target_pairs={{384,0},{0,128},{128,256},{256,384},{385,1},{1,129},{129,257},{257... | collective-permute-start | bytes 98312 | tf_op jit(solution)/shard_map/ppermute | solution.py:422
  26.1 7.4 %collective-permute-start.2 = (f32[64,128]{1,0:T(8,128)S(1)}, f32[64,128]{1,0:T(8,128)S(1)}, u32[]{:S(2)}, u32[]{:S(2)}) collective-permute-start(f32[64,128]{1,0:T(8,128)S(1)} %constant_dynamic-update-slice_fusion.n0), channel_id=1, source_target_pairs={{256,0},{384,128},{0,256},{128,384},{257,1},{385,129},{1,257},{129... | collective-permute-start | bytes 98312 | tf_op jit(solution)/shard_map/ppermute | solution.py:422
  30.5 5.0 %collective-permute-start.1 = (f32[64,128]{1,0:T(8,128)S(1)}, f32[64,128]{1,0:T(8,128)S(1)}, u32[]{:S(2)}, u32[]{:S(2)}) collective-permute-start(f32[64,128]{1,0:T(8,128)S(1)} %constant_dynamic-update-slice_fusion.n0), channel_id=1, source_target_pairs={{128,0},{256,128},{384,256},{0,384},{129,1},{257,129},{385,257},{1... | collective-permute-start | bytes 98312 | tf_op jit(solution)/shard_map/ppermute | solution.py:422
  50.0 47.6 %copy-start.1 = (f32[4,128]{1,0:T(4,128)S(1)}, f32[4,128]{1,0:T(4,128)}, u32[]{:S(2)}) copy-start(f32[4,128]{1,0:T(4,128)} %get-tuple-element.29.data) | copy-start | bytes 6148

commit v4 on v3

--- a/solution.py
+++ b/solution.py
@@ -170,20 +170,19 @@
     adjoint_terms(block, rows, msg, jnp.where(ids < 0.0, square, ids), zmsg)
 
 
-def select_sum(arrived, ids, named, pmsg, extra):
+def select_sum(arrived, ids, wanted, pmsg, extra):
     terms = jnp.concatenate([arrived[z * ZCH : z * ZCH + ENTRIES, :] for z in range(Z)], axis=0)
     high = terms.astype(BF16)
     rest = terms - high.astype(F32)
     mid = rest.astype(BF16)
     low = (rest - mid.astype(F32)).astype(BF16)
     step = lax.broadcasted_iota(jnp.int32, (OWN, BS), 0)
-    x_here, z_here, core_here = [lax.axis_index(axis) for axis in ROWS]
-    peers, names = [], []
-    for away in range(X):
-        for other in range(CORE):
-            x, core = (x_here + away) % X, (core_here + other) % CORE
-            peers.append(x * CORE + core)
-            names.append(named[away][other * ENTRIES : (other + 1) * ENTRIES, :])
+    z_here = lax.axis_index("z")
+    names = []
+    for x in range(X):
+        for core in range(CORE):
+            i = x * CORE + core
+            names.append(wanted[i * ENTRIES : (i + 1) * ENTRIES, :])
             names.append((((x * Z + z_here) * CORE + core) * OWN + step).astype(F32))
     names = jnp.concatenate(names, axis=0)
     pick = jnp.concatenate(
@@ -192,13 +191,12 @@
     sums = jnp.dot(pick, low, preferred_element_type=F32)
     sums = sums + jnp.dot(pick, mid, preferred_element_type=F32)
     sums = sums + jnp.dot(pick, high, preferred_element_type=F32)
-    for i, peer in enumerate(peers):
-        at = pl.multiple_of(peer * PCH, 8)
-        pmsg[pl.ds(at, WANT), :] = sums[i * WANT : (i + 1) * WANT]
-        pmsg[pl.ds(at + WANT, 8), :] = extra
-
-
-def first_select_kernel(arrived, n0, n1, n2, n3, pmsg, ids):
+    for i in range(N_PLANE):
+        pmsg[i * PCH : i * PCH + WANT, :] = sums[i * WANT : (i + 1) * WANT]
+        pmsg[i * PCH + WANT : (i + 1) * PCH, :] = extra
+
+
+def first_select_kernel(arrived, wanted, pmsg, ids):
     lane = lax.broadcasted_iota(jnp.int32, (1, BS), 1)
     extra = jnp.zeros((1, BS), F32)
     for t in range(Z // GROUPS):
@@ -210,14 +208,14 @@
             extra = extra + jnp.where(lane == (j + 1) % GROUPS * ENTRIES, line, 0.0)
         ids[t : t + 1, :] = row
     ids[Z // GROUPS : 8, :] = jnp.zeros((8 - Z // GROUPS, BS), F32)
-    select_sum(arrived, ids, (n0, n1, n2, n3), pmsg, jnp.broadcast_to(extra, (8, BS)))
-
-
-def select_kernel(arrived, n0, n1, n2, n3, ids, pmsg):
+    select_sum(arrived, ids, wanted, pmsg, jnp.broadcast_to(extra, (8, BS)))
+
+
+def select_kernel(arrived, wanted, ids, pmsg):
     extra = arrived[ENTRIES : ENTRIES + 1, :]
     for z in range(1, Z):
         extra = extra + arrived[z * ZCH + ENTRIES : z * ZCH + ZCH, :]
-    select_sum(arrived, ids, (n0, n1, n2, n3), pmsg, jnp.broadcast_to(extra, (8, BS)))
+    select_sum(arrived, ids, wanted, pmsg, jnp.broadcast_to(extra, (8, BS)))
 
 
 def plane_sum(arrived):
@@ -418,14 +416,13 @@
         **heavy,
     )(blocks, seismograms, signs, pattern, ownership)
     arrived = exchange(zmsg, "z", Z)
-    near = jnp.concatenate([named, lax.ppermute(named, "core", [(0, 1), (1, 0)])], axis=0)
-    named = [near] + [lax.ppermute(near, "x", [((i + d) % X, i) for i in range(X)]) for d in range(1, X)]
-    pmsg, ids = call(first_select_kernel, [pshape, row8], [VMEM] * 5)(arrived, *named)
+    wanted = lax.all_gather(named, PLANE, axis=0, tiled=True)
+    pmsg, ids = call(first_select_kernel, [pshape, row8], [VMEM] * 2)(arrived, wanted)
     v_raw, beta, ymsg = call(
         first_forward_kernel, [(WANT, BS), row8, (Y * 8, BS)], [VMEM] * 2, [acc], **heavy
     )(blocks, exchange(pmsg, PLANE, N_PLANE))
     rows_one, zmsg = call(adjoint_kernel, [row8, zshape], [VMEM] * 2, [msg], **heavy)(blocks, exchange(ymsg, "y", Y))
-    (pmsg,) = call(select_kernel, [pshape], [VMEM] * 6)(exchange(zmsg, "z", Z), *named, ids)
+    (pmsg,) = call(select_kernel, [pshape], [VMEM] * 3)(exchange(zmsg, "z", Z), wanted, ids)
     model_v, model_a, data_u, data_g, alpha, ymsg = call(
         second_forward_kernel,
         [(OWN, BS), (OWN, BS), row4, row4, row8, (N_PLANE * Y * PRODUCTS, BS)],

time: 129 us -> 124 us (0.961)
  starting transfers between devices: 29.1 us -> 15.8 us
  blocking collectives: 88.6 us -> 101 us
  waiting for transfers between devices: 2.18 us -> 0.01 us
    all_gather x0 -> x1, blocking collectives: none -> 14.1 us  [on_device(): wanted = lax.all_gather(named, PLANE, axis=0, tiled=True)]
    ppermute x4 -> x0, starting transfers between devices: 13.4 us -> none  [the longest x3 10.5 us: on_device(): lax.ppermute(near, 'x', [((i + d) % X, i) for i in range(X)])]
    all_to_all x3, blocking collectives: 50.9 us -> 46.8 us  [exchange(): lax.all_to_all(array.reshape(peers * n, 1, BS), axes, 0, 0, tiled=True)]
    all_to_all x3, blocking collectives: 37.7 us -> 39.9 us  [exchange(): lax.all_to_all(array.reshape(peers, n, BS), axes, 0, 0, tiled=True)]
    ppermute x4 -> x0, waiting for transfers between devices: 2.17 us -> none  [the longest x3 1.87 us: on_device(): lax.ppermute(near, 'x', [((i + d) % X, i) for i in range(X)])]
  transfers between devices with their start and end apart: 5 -> 1, of which waited for: 2 -> 0; matrix products, arithmetic and copies ran while one was open for 1% -> 0% of each run, Pallas kernels for 0% -> 0%
where the time goes in v4:
time: 124 us
  blocking collectives  101 us (81%)
  starting transfers between devices  15.8 us (13%)
  Pallas kernels  6.7 us (5%)
    all_to_all x3, blocking collectives, exchange(): lax.all_to_all(array.reshape(peers * n, 1, BS), axes, 0, 0, tiled=True)  46.8 us
    all_to_all x3, blocking collectives, exchange(): lax.all_to_all(array.reshape(peers, n, BS), axes, 0, 0, tiled=True)  39.9 us
    all_to_all x1, starting transfers between devices, exchange(): lax.all_to_all(array.reshape(peers * n, 1, BS), axes, 0, 0, tiled=True)  15.8 us
    all_gather x1, blocking collectives, on_device(): wanted = lax.all_gather(named, PLANE, axis=0, tiled=True)  14.1 us
    pallas_call x1, Pallas kernels, on_device(): call(first_kernel, [row4, zshape, (ENTRIES, BS)], [HBM] * 5, [msg, pltpu....  2.69 us
  transfers between devices with their start and end apart: 1, of which 0 were waited for; matrix products, arithmetic and copies ran while one was open for 0% of the time, Pallas kernels for 0%

profile of v4, /device:TPU:1, one launch (start us, length us, event | category | flops | bytes accessed | tf_op | source)
XLA Modules:
  0.0 124.0 jit_solution(5048932348405825910)
XLA Ops:
  0.6 0.0 copy-start
  0.6 2.7 %shard_map.68 = (f32[4,128]{1,0:T(4,128)}, f32[528,128]{1,0:T(8,128)}, f32[32,128]{1,0:T(8,128)}) custom-call(f32[4,8,128,128]{3,2,1,0:T(8,128)} %bitcast.25, f32[4,512]{1,0:T(4,128)} %seis.1, s32[4,512]{1,0:T(4,128)} %signs.1, s32[4,8]{1,0:T(4,128)} %pat.1, s32[2048]{0:T(1024)} %own.1), custom_call_target="tpu_custom_call" | custom-call | flops 1048576 | bytes 2097152 | tf_op jit(solution)/shard_map/pallas_call | solution.py:401
  3.3 15.8 %all-to-all-start = ((f32[528,1,128]{2,1,0:T(1,128)}), f32[528,1,128]{2,1,0:T(1,128)S(1)}, u32[]{:S(2)}, u32[]{:S(2)}) async-start(f32[528,1,128]{2,1,0:T(1,128)} %bitcast.42), calls=%async_computation | async-start | bytes 540672 | tf_op jit(solution)/shard_map/all_to_all | solution.py:380
  19.1 14.1 %all_gather.3.wanted = f32[256,128]{1,0:T(8,128)S(1)} all-gather(f32[32,128]{1,0:T(8,128)} %get-tuple-element.23), channel_id=1, replica_groups=mesh['x'=4,'z'=16,'core'=2,'y'=4] {'x','core'}, dimensions={0}, use_global_device_ids=true | all-gather | bytes 147456 | tf_op jit(solution)/shard_map/all_gather | solution.py:419
  33.2 0.0 all-to-all-done
  33.2 0.5 shard_map.69
  33.7 15.7 %all_to_all.35 = f32[8,56,128]{2,1,0:T(8,128)S(1)} all-to-all(f32[8,56,128]{2,1,0:T(8,128)S(1)} %bitcast.36), channel_id=1, replica_groups=mesh['x'=4,'z'=16,'core'=2,'y'=4] {'x','core'}, dimensions={0} | all-to-all | bytes 458752 | tf_op jit(solution)/shard_map/all_to_all | solution.py:379
  49.4 0.0 copy-done
  49.4 0.5 shard_map.70
  50.0 0.0 copy-start.1
  50.0 8.3 %all_to_all.36 = f32[4,8,128]{2,1,0:T(8,128)S(1)} all-to-all(f32[4,8,128]{2,1,0:T(8,128)S(1)} %bitcast.40), channel_id=1, replica_groups=mesh['x'=4,'z'=16,'core'=2,'y'=4] {'y'}, dimensions={0} | all-to-all | bytes 32768 | tf_op jit(solution)/shard_map/all_to_all | solution.py:379
  58.3 0.3 shard_map.71
  58.5 18.5 %all_to_all.37 = f32[528,1,128]{2,1,0:T(1,128)S(1)} all-to-all(f32[528,1,128]{2,1,0:T(1,128)S(1)} %bitcast.35), channel_id=1, replica_groups=mesh['x'=4,'z'=16,'core'=2,'y'=4] {'z'}, dimensions={0} | all-to-all | bytes 540672 | tf_op jit(solution)/shard_map/all_to_all | solution.py:380
  77.1 0.5 shard_map.72
  77.5 15.9 %all_to_all.38 = f32[8,56,128]{2,1,0:T(8,128)S(1)} all-to-all(f32[8,56,128]{2,1,0:T(8,128)S(1)} %bitcast.32), channel_id=1, replica_groups=mesh['x'=4,'z'=16,'core'=2,'y'=4] {'x','core'}, dimensions={0} | all-to-all | bytes 458752 | tf_op jit(solution)/shard_map/all_to_all | solution.py:379
  93.5 0.0 copy-done.1
  93.5 0.6 shard_map.73
  94.1 12.2 %all_to_all.39 = f32[384,1,128]{2,1,0:T(1,128)S(1)} all-to-all(f32[384,1,128]{2,1,0:T(1,128)S(1)} %bitcast.37), channel_id=1, replica_groups=mesh['x'=4,'z'=16,'core'=2,'y'=4] {'x','core','y'}, dimensions={0} | all-to-all | bytes 393216 | tf_op jit(solution)/shard_map/all_to_all | solution.py:380
  106.2 0.7 shard_map.74
  107.0 16.1 %all_to_all.40 = f32[16,1,128]{2,1,0:T(1,128)S(1)} all-to-all(f32[16,1,128]{2,1,0:T(1,128)S(1)} %bitcast.41), channel_id=1, replica_groups=mesh['x'=4,'z'=16,'core'=2,'y'=4] {'z'}, dimensions={0} | all-to-all | bytes 16384 | tf_op jit(solution)/shard_map/all_to_all | solution.py:380
  123.1 0.9 shard_map.75
Async XLA Ops:
  0.6 48.8 %copy-start = (f32[1,4,8,128,128]{4,3,2,1,0:T(8,128)S(1)}, f32[1,4,8,128,128]{4,3,2,1,0:T(8,128)}, u32[]{:S(2)}) copy-start(f32[1,4,8,128,128]{4,3,2,1,0:T(8,128)} %param.5) | copy-start | bytes 6291460
  3.3 29.9 %all-to-all-start = ((f32[528,1,128]{2,1,0:T(1,128)}), f32[528,1,128]{2,1,0:T(1,128)S(1)}, u32[]{:S(2)}, u32[]{:S(2)}) async-start(f32[528,1,128]{2,1,0:T(1,128)} %bitcast.42), calls=%async_computation | async-start | bytes 540672 | tf_op jit(solution)/shard_map/all_to_all | solution.py:380
  50.0 43.5 %copy-start.1 = (f32[4,128]{1,0:T(4,128)S(1)}, f32[4,128]{1,0:T(4,128)}, u32[]{:S(2)}) copy-start(f32[4,128]{1,0:T(4,128)} %get-tuple-element.29.data) | copy-start | bytes 6148

commit v5 on v4

--- a/solution.py
+++ b/solution.py
@@ -23,8 +23,9 @@
 OWN = 16
 WANT = ENTRIES + OWN
 ZCH = ENTRIES + 1
-PCH = WANT + 8
+PCH = WANT + 1
 PRODUCTS = 12
+PART = 2
 GROUPS = BS // ENTRIES
 DOTS = 9
 
@@ -101,14 +102,16 @@
     return fold_rows(two_prod(a, b))
 
 
-def adjoint_terms(block, u_rows, msg, extra, zmsg):
+def adjoint_terms(block, u_rows, msg, extra):
     for r in range(RB):
         spread = jnp.transpose(jnp.broadcast_to(u_rows[r], (BS, BS)))
-        row = block(r)
         for k in range(NNZ):
             e = r * NNZ + k
-            msg[e : e + 1, :] = jnp.sum(row[k] * spread, axis=0, keepdims=True)
+            msg[e : e + 1, :] = jnp.sum(block(r, k) * spread, axis=0, keepdims=True)
     msg[ENTRIES : ENTRIES + 1, :] = extra
+
+
+def spread_message(msg, zmsg):
     whole = msg[0:ZCH, :]
     for z in range(Z):
         zmsg[z * ZCH : (z + 1) * ZCH, :] = whole
@@ -138,7 +141,10 @@
         pltpu.make_async_copy(src, dst, sems.at[i])
         for i, (src, dst) in enumerate(((pat, pat_s), (own, own_s), (seis, seis_v), (signs, signs_v)))
     ]
-    large = [pltpu.make_async_copy(blocks.at[r], held.at[r], block_sems.at[r]) for r in range(RB)]
+    large = [
+        pltpu.make_async_copy(blocks.at[pl.ds(r, PART)], held.at[pl.ds(r, PART)], block_sems.at[r // PART])
+        for r in range(0, RB, PART)
+    ]
     for copy in small + large:
         copy.start()
     small[2].wait()
@@ -163,11 +169,13 @@
     named[...] = col.astype(F32)
     ids = row.astype(F32)
 
-    def block(r):
-        large[r].wait()
-        return [held[r, k] for k in range(NNZ)]
-
-    adjoint_terms(block, rows, msg, jnp.where(ids < 0.0, square, ids), zmsg)
+    def block(r, k):
+        if k == 0 and r % PART == 0:
+            large[r // PART].wait()
+        return held[r, k]
+
+    adjoint_terms(block, rows, msg, jnp.where(ids < 0.0, square, ids))
+    spread_message(msg, zmsg)
 
 
 def select_sum(arrived, ids, wanted, pmsg, extra):
@@ -193,7 +201,7 @@
     sums = sums + jnp.dot(pick, high, preferred_element_type=F32)
     for i in range(N_PLANE):
         pmsg[i * PCH : i * PCH + WANT, :] = sums[i * WANT : (i + 1) * WANT]
-        pmsg[i * PCH + WANT : (i + 1) * PCH, :] = extra
+        pmsg[i * PCH + WANT : (i + 1) * PCH, :] = extra[0:1, :]
 
 
 def first_select_kernel(arrived, wanted, pmsg, ids):
@@ -252,7 +260,8 @@
         total = total + arrived[y * 8 : (y + 1) * 8, :]
     rows_out[...] = total
     rows = [total[r : r + 1, :] for r in range(RB)]
-    adjoint_terms(lambda r: [blocks[r, k] for k in range(NNZ)], rows, msg, total[RB : RB + 1, :], zmsg)
+    adjoint_terms(lambda r, k: blocks[r, k], rows, msg, total[RB : RB + 1, :])
+    spread_message(msg, zmsg)
 
 
 def second_forward_kernel(
@@ -410,7 +419,7 @@
             pltpu.SMEM(pattern.shape, jnp.int32),
             pltpu.SMEM(ownership.shape, jnp.int32),
             pltpu.SemaphoreType.DMA((4,)),
-            pltpu.SemaphoreType.DMA((RB,)),
+            pltpu.SemaphoreType.DMA((RB // PART,)),
         ],
         vmem=59 * 1024 * 1024,
         **heavy,

time: 124 us -> 124 us (level)
    all_to_all x3 -> x1, blocking collectives: 39.9 us -> 8.33 us  [exchange(): lax.all_to_all(array.reshape(peers, n, BS), axes, 0, 0, tiled=True)]
    all_to_all x3 -> x5, blocking collectives: 46.8 us -> 77.9 us  [exchange(): lax.all_to_all(array.reshape(peers * n, 1, BS), axes, 0, 0, tiled=True)]
where the time goes in v5:
time: 124 us; the launch traced here: 123 us
  blocking collectives  100 us (81%)
  starting transfers between devices  15.8 us (13%)
  Pallas kernels  6.62 us (5%)
    all_to_all x5, blocking collectives, exchange(): lax.all_to_all(array.reshape(peers * n, 1, BS), axes, 0, 0, tiled=True)  77.9 us
    all_to_all x1, starting transfers between devices, exchange(): lax.all_to_all(array.reshape(peers * n, 1, BS), axes, 0, 0, tiled=True)  15.8 us
    all_gather x1, blocking collectives, on_device(): wanted = lax.all_gather(named, PLANE, axis=0, tiled=True)  14.1 us
    all_to_all x1, blocking collectives, exchange(): lax.all_to_all(array.reshape(peers, n, BS), axes, 0, 0, tiled=True)  8.33 us
    pallas_call x1, Pallas kernels, on_device(): call(first_kernel, [row4, zshape, (ENTRIES, BS)], [HBM] * 5, [msg, pltpu....  2.62 us
  transfers between devices with their start and end apart: 1, of which 0 were waited for; matrix products, arithmetic and copies ran while one was open for 0% of the time, Pallas kernels for 0%

profile of v5, /device:TPU:1, one launch (start us, length us, event | category | flops | bytes accessed | tf_op | source)
XLA Modules:
  0.0 123.4 jit_solution(16781376377400983798)
XLA Ops:
  0.6 0.0 copy-start
  0.6 2.6 %shard_map.68 = (f32[4,128]{1,0:T(4,128)}, f32[528,128]{1,0:T(8,128)}, f32[32,128]{1,0:T(8,128)}) custom-call(f32[4,8,128,128]{3,2,1,0:T(8,128)} %bitcast.29, f32[4,512]{1,0:T(4,128)} %seis.1, s32[4,512]{1,0:T(4,128)} %signs.1, s32[4,8]{1,0:T(4,128)} %pat.1, s32[2048]{0:T(1024)} %own.1), custom_call_target="tpu_custom_call" | custom-call | flops 1048576 | bytes 2097152 | tf_op jit(solution)/shard_map/pallas_call | solution.py:410
  3.3 15.8 %all-to-all-start = ((f32[528,1,128]{2,1,0:T(1,128)}), f32[528,1,128]{2,1,0:T(1,128)S(1)}, u32[]{:S(2)}, u32[]{:S(2)}) async-start(f32[528,1,128]{2,1,0:T(1,128)} %bitcast.46), calls=%async_computation | async-start | bytes 540672 | tf_op jit(solution)/shard_map/all_to_all | solution.py:389
  19.0 14.1 %all_gather.3.wanted = f32[256,128]{1,0:T(8,128)S(1)} all-gather(f32[32,128]{1,0:T(8,128)} %get-tuple-element.23), channel_id=1, replica_groups=mesh['x'=4,'z'=16,'core'=2,'y'=4] {'x','core'}, dimensions={0}, use_global_device_ids=true | all-gather | bytes 147456 | tf_op jit(solution)/shard_map/all_gather | solution.py:428
  33.1 0.0 all-to-all-done
  33.1 0.5 shard_map.69
  33.6 15.4 %all_to_all.35 = f32[392,1,128]{2,1,0:T(1,128)S(1)} all-to-all(f32[392,1,128]{2,1,0:T(1,128)S(1)} %bitcast.40), channel_id=1, replica_groups=mesh['x'=4,'z'=16,'core'=2,'y'=4] {'x','core'}, dimensions={0} | all-to-all | bytes 401408 | tf_op jit(solution)/shard_map/all_to_all | solution.py:389
  49.1 0.0 copy-done
  49.1 0.5 shard_map.70
  49.6 0.0 copy-start.1
  49.6 8.3 %all_to_all.36 = f32[4,8,128]{2,1,0:T(8,128)S(1)} all-to-all(f32[4,8,128]{2,1,0:T(8,128)S(1)} %bitcast.44), channel_id=1, replica_groups=mesh['x'=4,'z'=16,'core'=2,'y'=4] {'y'}, dimensions={0} | all-to-all | bytes 32768 | tf_op jit(solution)/shard_map/all_to_all | solution.py:388
  57.9 0.3 shard_map.71
  58.2 18.5 %all_to_all.37 = f32[528,1,128]{2,1,0:T(1,128)S(1)} all-to-all(f32[528,1,128]{2,1,0:T(1,128)S(1)} %bitcast.39), channel_id=1, replica_groups=mesh['x'=4,'z'=16,'core'=2,'y'=4] {'z'}, dimensions={0} | all-to-all | bytes 540672 | tf_op jit(solution)/shard_map/all_to_all | solution.py:389
  76.7 0.5 shard_map.72
  77.2 15.6 %all_to_all.38 = f32[392,1,128]{2,1,0:T(1,128)S(1)} all-to-all(f32[392,1,128]{2,1,0:T(1,128)S(1)} %bitcast.36), channel_id=1, replica_groups=mesh['x'=4,'z'=16,'core'=2,'y'=4] {'x','core'}, dimensions={0} | all-to-all | bytes 401408 | tf_op jit(solution)/shard_map/all_to_all | solution.py:389
  92.8 0.0 copy-done.1
  92.8 0.6 shard_map.73
  93.4 12.1 %all_to_all.39 = f32[384,1,128]{2,1,0:T(1,128)S(1)} all-to-all(f32[384,1,128]{2,1,0:T(1,128)S(1)} %bitcast.41), channel_id=1, replica_groups=mesh['x'=4,'z'=16,'core'=2,'y'=4] {'x','core','y'}, dimensions={0} | all-to-all | bytes 393216 | tf_op jit(solution)/shard_map/all_to_all | solution.py:389
  105.5 0.7 shard_map.74
  106.2 16.2 %all_to_all.40 = f32[16,1,128]{2,1,0:T(1,128)S(1)} all-to-all(f32[16,1,128]{2,1,0:T(1,128)S(1)} %bitcast.45), channel_id=1, replica_groups=mesh['x'=4,'z'=16,'core'=2,'y'=4] {'z'}, dimensions={0} | all-to-all | bytes 16384 | tf_op jit(solution)/shard_map/all_to_all | solution.py:389
  122.5 0.9 shard_map.75
Async XLA Ops:
  0.6 48.4 %copy-start = (f32[1,4,8,128,128]{4,3,2,1,0:T(8,128)S(1)}, f32[1,4,8,128,128]{4,3,2,1,0:T(8,128)}, u32[]{:S(2)}) copy-start(f32[1,4,8,128,128]{4,3,2,1,0:T(8,128)} %param.5) | copy-start | bytes 6291460
  3.3 29.9 %all-to-all-start = ((f32[528,1,128]{2,1,0:T(1,128)}), f32[528,1,128]{2,1,0:T(1,128)S(1)}, u32[]{:S(2)}, u32[]{:S(2)}) async-start(f32[528,1,128]{2,1,0:T(1,128)} %bitcast.46), calls=%async_computation | async-start | bytes 540672 | tf_op jit(solution)/shard_map/all_to_all | solution.py:389
  49.6 43.2 %copy-start.1 = (f32[4,128]{1,0:T(4,128)S(1)}, f32[4,128]{1,0:T(4,128)}, u32[]{:S(2)}) copy-start(f32[4,128]{1,0:T(4,128)} %get-tuple-element.29.data) | copy-start | bytes 6148

commit v6 on v5

--- a/solution.py
+++ b/solution.py
@@ -117,21 +117,15 @@
         zmsg[z * ZCH : (z + 1) * ZCH, :] = whole
 
 
-def forward_rows(blocks, chosen, acc):
+def forward_rows(blocks, chosen):
+    rows = []
     for r in range(RB):
         total = blocks[r, 0] * chosen[r * NNZ : r * NNZ + 1, :]
         for k in range(1, NNZ):
             e = r * NNZ + k
             total = total + blocks[r, k] * chosen[e : e + 1, :]
-        acc[r * BS : (r + 1) * BS, :] = total
-    sums = lax.dot_general(
-        jnp.ones((8, BS), F32),
-        acc[...],
-        (((1,), (1,)), ((), ())),
-        precision=lax.Precision.HIGHEST,
-        preferred_element_type=F32,
-    )
-    return [sums[0:1, r * BS : (r + 1) * BS] for r in range(RB)]
+        rows.append(jnp.sum(jnp.transpose(total), axis=0, keepdims=True))
+    return rows
 
 
 def first_kernel(
@@ -197,8 +191,8 @@
         [jnp.where(names == ids[t : t + 1, :], 1.0, 0.0).astype(BF16) for t in range(Z * ENTRIES // BS)], axis=1
     )
     sums = jnp.dot(pick, low, preferred_element_type=F32)
-    sums = sums + jnp.dot(pick, mid, preferred_element_type=F32)
-    sums = sums + jnp.dot(pick, high, preferred_element_type=F32)
+    both = jnp.dot(pick, jnp.concatenate([mid, high], axis=1), preferred_element_type=F32)
+    sums = sums + both[:, :BS] + both[:, BS:]
     for i in range(N_PLANE):
         pmsg[i * PCH : i * PCH + WANT, :] = sums[i * WANT : (i + 1) * WANT]
         pmsg[i * PCH + WANT : (i + 1) * PCH, :] = extra[0:1, :]
@@ -240,12 +234,12 @@
     return jnp.sum(total, axis=1, keepdims=True)
 
 
-def first_forward_kernel(blocks, arrived, v_raw, beta, ymsg, acc):
+def first_forward_kernel(blocks, arrived, v_raw, beta, ymsg):
     beta_one = jnp.sqrt(plane_extra(arrived) + EPS)
     v = plane_sum(arrived) / beta_one
     v_raw[...] = v
     beta[...] = jnp.broadcast_to(beta_one, (8, BS))
-    rows = forward_rows(blocks, v, acc)
+    rows = forward_rows(blocks, v)
     own = v[ENTRIES:WANT]
     extra = jnp.sum(own * own, axis=0, keepdims=True)
     for y in range(Y):
@@ -265,7 +259,7 @@
 
 
 def second_forward_kernel(
-    blocks, arrived, v_raw, data, beta, rows_one, model_v, model_a, data_u, data_g, alpha, ymsg, acc, msg
+    blocks, arrived, v_raw, data, beta, rows_one, model_v, model_a, data_u, data_g, alpha, ymsg, msg
 ):
     alpha_one = jnp.sqrt(plane_extra(arrived) + EPS)
     v = v_raw[...]
@@ -275,7 +269,7 @@
     u = g - alpha_one * (data[...] / beta[0:1, 0:1])
     data_u[...] = u
     alpha[...] = jnp.broadcast_to(alpha_one, (8, BS))
-    rows = forward_rows(blocks, a, acc)
+    rows = forward_rows(blocks, a)
     a_own = a[ENTRIES:WANT]
     v_own = v[ENTRIES:WANT] / alpha_one
     model_a[...] = a_own
@@ -315,8 +309,8 @@
     u = u_all[...]
     g = g_all[...]
     pairs = [dot_rows(u, u), dot_rows(q, q), dot_rows(q, g), dot_rows(q, u), dot_rows(g, g), dot_rows(g, u)]
-    high[...] = jnp.zeros((16, BS), F32)
-    low[...] = jnp.zeros((16, BS), F32)
+    high[...] = jnp.zeros((BS, BS), F32)
+    low[...] = jnp.zeros((BS, BS), F32)
     for i, pair in enumerate(pairs):
         high[i : i + 1, :] = pair[0]
         low[i : i + 1, :] = pair[1]
@@ -324,15 +318,8 @@
         model = [dd_add(model[i], model[i + 1]) for i in range(0, len(model), 2)]
     high[6:9, :] = model[0][0]
     low[6:9, :] = model[0][1]
-    pair = (high[...], low[...])
-    step = BS // 2
-    while step:
-        pair = dd_add(pair, (pltpu.roll(pair[0], step, 1), pltpu.roll(pair[1], step, 1)))
-        step //= 2
-    lane = lax.broadcasted_iota(jnp.int32, (16, BS), 1)
-    sub = lax.broadcasted_iota(jnp.int32, (16, BS), 0)
-    line = jnp.where(lane == sub, pair[0], 0.0) + jnp.where(lane == sub + 64, pair[1], 0.0)
-    line = jnp.sum(line, axis=0, keepdims=True)
+    pair = fold_rows((jnp.transpose(high[...]), jnp.transpose(low[...])))
+    line = pair[0] + pltpu.roll(pair[1], BS // 2, 1)
     rmsg[...] = jnp.broadcast_to(line, (Z, BS))
 
 
@@ -341,12 +328,12 @@
     pair = fold_rows((total, jnp.zeros_like(total)))
     lane = lax.broadcasted_iota(jnp.int32, (1, BS), 1)
 
-    def take(line, i):
-        return jnp.sum(jnp.where(lane == i, line, 0.0), axis=1, keepdims=True)
+    rest = jnp.where(lane < BS // 2, pair[1], pair[0] + pair[1])
 
     def dot(i):
-        low = take(pair[1], i) + (take(pair[0], 64 + i) + take(pair[1], 64 + i))
-        return dd_add((take(pair[0], i), jnp.zeros((1, 1), F32)), (low, jnp.zeros((1, 1), F32)))
+        top = jnp.sum(jnp.where(lane == i, pair[0], 0.0), axis=1, keepdims=True)
+        low = jnp.sum(jnp.where(lane % (BS // 2) == i, rest, 0.0), axis=1, keepdims=True)
+        return two_sum(top, low)
 
     uu, qq, qg, qu, gg, gu, aa, av, vv = [dot(i) for i in range(DOTS)]
     beta_one = beta[0:1, 0:1]
@@ -402,7 +389,6 @@
     blocks = frechet[0]
     size = blocks.size
     msg = pltpu.VMEM((ENTRIES + 8, BS), F32)
-    acc = pltpu.VMEM((RB * BS, BS), F32)
     row4, row8 = (RB, BS), (8, BS)
     zshape, pshape = (Z * ZCH, BS), (N_PLANE * PCH, BS)
     heavy = dict(flops=2 * size, moved=4 * size)
@@ -428,7 +414,7 @@
     wanted = lax.all_gather(named, PLANE, axis=0, tiled=True)
     pmsg, ids = call(first_select_kernel, [pshape, row8], [VMEM] * 2)(arrived, wanted)
     v_raw, beta, ymsg = call(
-        first_forward_kernel, [(WANT, BS), row8, (Y * 8, BS)], [VMEM] * 2, [acc], **heavy
+        first_forward_kernel, [(WANT, BS), row8, (Y * 8, BS)], [VMEM] * 2, **heavy
     )(blocks, exchange(pmsg, PLANE, N_PLANE))
     rows_one, zmsg = call(adjoint_kernel, [row8, zshape], [VMEM] * 2, [msg], **heavy)(blocks, exchange(ymsg, "y", Y))
     (pmsg,) = call(select_kernel, [pshape], [VMEM] * 3)(exchange(zmsg, "z", Z), wanted, ids)
@@ -436,14 +422,14 @@
         second_forward_kernel,
         [(OWN, BS), (OWN, BS), row4, row4, row8, (N_PLANE * Y * PRODUCTS, BS)],
         [VMEM] * 6,
-        [acc, pltpu.VMEM((2 * PRODUCTS, BS), F32)],
+        [pltpu.VMEM((2 * PRODUCTS, BS), F32)],
         **heavy,
     )(blocks, exchange(pmsg, PLANE, N_PLANE), v_raw, data, beta, rows_one)
     data_q, rmsg = call(
         products_kernel,
         [row4, (Z, BS)],
         [VMEM],
-        [pltpu.VMEM((N_PLANE * RB, BS), F32)] * 3 + [pltpu.VMEM((16, BS), F32)] * 2,
+        [pltpu.VMEM((N_PLANE * RB, BS), F32)] * 3 + [pltpu.VMEM((BS, BS), F32)] * 2,
     )(exchange(ymsg, PLANE + ("y",), N_PLANE * Y))
     model, data_dir = call(last_kernel, [(OWN, BS), row4], [VMEM] * 8)(
         exchange(rmsg, "z", Z), beta, alpha, model_v, model_a, data_u, data_g, data_q

time: 124 us -> 123 us (level)
  no operation moved by 1% of the time
where the time goes in v6:
time: 123 us; the launch traced here: 122 us
  blocking collectives  100 us (81%)
  starting transfers between devices  15.8 us (13%)
  Pallas kernels  5.61 us (5%)
    all_to_all x5, blocking collectives, exchange(): lax.all_to_all(array.reshape(peers * n, 1, BS), axes, 0, 0, tiled=True)  77.8 us
    all_to_all x1, starting transfers between devices, exchange(): lax.all_to_all(array.reshape(peers * n, 1, BS), axes, 0, 0, tiled=True)  15.8 us
    all_gather x1, blocking collectives, on_device(): wanted = lax.all_gather(named, PLANE, axis=0, tiled=True)  14.1 us
    all_to_all x1, blocking collectives, exchange(): lax.all_to_all(array.reshape(peers, n, BS), axes, 0, 0, tiled=True)  8.19 us
    pallas_call x1, Pallas kernels, on_device(): call(first_kernel, [row4, zshape, (ENTRIES, BS)], [HBM] * 5, [msg, pltpu....  2.62 us
  transfers between devices with their start and end apart: 1, of which 0 were waited for; matrix products, arithmetic and copies ran while one was open for 0% of the time, Pallas kernels for 0%

profile of v6, /device:TPU:1, one launch (start us, length us, event | category | flops | bytes accessed | tf_op | source)
XLA Modules:
  0.0 122.2 jit_solution(2238460513007917347)
XLA Ops:
  0.6 0.0 copy-start
  0.6 2.6 %shard_map.68 = (f32[4,128]{1,0:T(4,128)}, f32[528,128]{1,0:T(8,128)}, f32[32,128]{1,0:T(8,128)}) custom-call(f32[4,8,128,128]{3,2,1,0:T(8,128)} %bitcast.29, f32[4,512]{1,0:T(4,128)} %seis.1, s32[4,512]{1,0:T(4,128)} %signs.1, s32[4,8]{1,0:T(4,128)} %pat.1, s32[2048]{0:T(1024)} %own.1), custom_call_target="tpu_custom_call" | custom-call | flops 1048576 | bytes 2097152 | tf_op jit(solution)/shard_map/pallas_call | solution.py:396
  3.3 15.8 %all-to-all-start = ((f32[528,1,128]{2,1,0:T(1,128)}), f32[528,1,128]{2,1,0:T(1,128)S(1)}, u32[]{:S(2)}, u32[]{:S(2)}) async-start(f32[528,1,128]{2,1,0:T(1,128)} %bitcast.46), calls=%async_computation | async-start | bytes 540672 | tf_op jit(solution)/shard_map/all_to_all | solution.py:376
  19.0 14.1 %all_gather.3.wanted = f32[256,128]{1,0:T(8,128)S(1)} all-gather(f32[32,128]{1,0:T(8,128)} %get-tuple-element.23), channel_id=1, replica_groups=mesh['x'=4,'z'=16,'core'=2,'y'=4] {'x','core'}, dimensions={0}, use_global_device_ids=true | all-gather | bytes 147456 | tf_op jit(solution)/shard_map/all_gather | solution.py:414
  33.1 0.0 all-to-all-done
  33.1 0.4 shard_map.69
  33.5 15.4 %all_to_all.35 = f32[392,1,128]{2,1,0:T(1,128)S(1)} all-to-all(f32[392,1,128]{2,1,0:T(1,128)S(1)} %bitcast.40), channel_id=1, replica_groups=mesh['x'=4,'z'=16,'core'=2,'y'=4] {'x','core'}, dimensions={0} | all-to-all | bytes 401408 | tf_op jit(solution)/shard_map/all_to_all | solution.py:376
  49.0 0.0 copy-done
  49.0 0.3 shard_map.70
  49.3 0.0 copy-start.1
  49.3 8.2 %all_to_all.36 = f32[4,8,128]{2,1,0:T(8,128)S(1)} all-to-all(f32[4,8,128]{2,1,0:T(8,128)S(1)} %bitcast.44), channel_id=1, replica_groups=mesh['x'=4,'z'=16,'core'=2,'y'=4] {'y'}, dimensions={0} | all-to-all | bytes 32768 | tf_op jit(solution)/shard_map/all_to_all | solution.py:375
  57.5 0.3 shard_map.71
  57.7 18.5 %all_to_all.37 = f32[528,1,128]{2,1,0:T(1,128)S(1)} all-to-all(f32[528,1,128]{2,1,0:T(1,128)S(1)} %bitcast.39), channel_id=1, replica_groups=mesh['x'=4,'z'=16,'core'=2,'y'=4] {'z'}, dimensions={0} | all-to-all | bytes 540672 | tf_op jit(solution)/shard_map/all_to_all | solution.py:376
  76.2 0.4 shard_map.72
  76.6 15.6 %all_to_all.38 = f32[392,1,128]{2,1,0:T(1,128)S(1)} all-to-all(f32[392,1,128]{2,1,0:T(1,128)S(1)} %bitcast.36), channel_id=1, replica_groups=mesh['x'=4,'z'=16,'core'=2,'y'=4] {'x','core'}, dimensions={0} | all-to-all | bytes 401408 | tf_op jit(solution)/shard_map/all_to_all | solution.py:376
  92.2 0.0 copy-done.1
  92.2 0.4 shard_map.73
  92.5 12.1 %all_to_all.39 = f32[384,1,128]{2,1,0:T(1,128)S(1)} all-to-all(f32[384,1,128]{2,1,0:T(1,128)S(1)} %bitcast.41), channel_id=1, replica_groups=mesh['x'=4,'z'=16,'core'=2,'y'=4] {'x','core','y'}, dimensions={0} | all-to-all | bytes 393216 | tf_op jit(solution)/shard_map/all_to_all | solution.py:376
  104.7 0.4 shard_map.74
  105.1 16.2 %all_to_all.40 = f32[16,1,128]{2,1,0:T(1,128)S(1)} all-to-all(f32[16,1,128]{2,1,0:T(1,128)S(1)} %bitcast.45), channel_id=1, replica_groups=mesh['x'=4,'z'=16,'core'=2,'y'=4] {'z'}, dimensions={0} | all-to-all | bytes 16384 | tf_op jit(solution)/shard_map/all_to_all | solution.py:376
  121.3 0.9 shard_map.75
Async XLA Ops:
  0.6 48.3 %copy-start = (f32[1,4,8,128,128]{4,3,2,1,0:T(8,128)S(1)}, f32[1,4,8,128,128]{4,3,2,1,0:T(8,128)}, u32[]{:S(2)}) copy-start(f32[1,4,8,128,128]{4,3,2,1,0:T(8,128)} %param.5) | copy-start | bytes 6291460
  3.3 29.9 %all-to-all-start = ((f32[528,1,128]{2,1,0:T(1,128)}), f32[528,1,128]{2,1,0:T(1,128)S(1)}, u32[]{:S(2)}, u32[]{:S(2)}) async-start(f32[528,1,128]{2,1,0:T(1,128)} %bitcast.46), calls=%async_computation | async-start | bytes 540672 | tf_op jit(solution)/shard_map/all_to_all | solution.py:376
  49.3 42.9 %copy-start.1 = (f32[4,128]{1,0:T(4,128)S(1)}, f32[4,128]{1,0:T(4,128)}, u32[]{:S(2)}) copy-start(f32[4,128]{1,0:T(4,128)} %get-tuple-element.29.data) | copy-start | bytes 6148

commit v7 on v6

--- a/solution.py
+++ b/solution.py
@@ -25,7 +25,7 @@
 ZCH = ENTRIES + 1
 PCH = WANT + 1
 PRODUCTS = 12
-PART = 2
+PART = 4
 GROUPS = BS // ENTRIES
 DOTS = 9
 
@@ -194,8 +194,9 @@
     both = jnp.dot(pick, jnp.concatenate([mid, high], axis=1), preferred_element_type=F32)
     sums = sums + both[:, :BS] + both[:, BS:]
     for i in range(N_PLANE):
-        pmsg[i * PCH : i * PCH + WANT, :] = sums[i * WANT : (i + 1) * WANT]
-        pmsg[i * PCH + WANT : (i + 1) * PCH, :] = extra[0:1, :]
+        to = i % CORE * X + i // CORE
+        pmsg[to * PCH : to * PCH + WANT, :] = sums[i * WANT : (i + 1) * WANT]
+        pmsg[to * PCH + WANT : (to + 1) * PCH, :] = extra[0:1, :]
 
 
 def first_select_kernel(arrived, wanted, pmsg, ids):
@@ -415,7 +416,7 @@
     pmsg, ids = call(first_select_kernel, [pshape, row8], [VMEM] * 2)(arrived, wanted)
     v_raw, beta, ymsg = call(
         first_forward_kernel, [(WANT, BS), row8, (Y * 8, BS)], [VMEM] * 2, **heavy
-    )(blocks, exchange(pmsg, PLANE, N_PLANE))
+    )(blocks, exchange(pmsg, ("core", "x"), N_PLANE))
     rows_one, zmsg = call(adjoint_kernel, [row8, zshape], [VMEM] * 2, [msg], **heavy)(blocks, exchange(ymsg, "y", Y))
     (pmsg,) = call(select_kernel, [pshape], [VMEM] * 3)(exchange(zmsg, "z", Z), wanted, ids)
     model_v, model_a, data_u, data_g, alpha, ymsg = call(
@@ -424,7 +425,7 @@
         [VMEM] * 6,
         [pltpu.VMEM((2 * PRODUCTS, BS), F32)],
         **heavy,
-    )(blocks, exchange(pmsg, PLANE, N_PLANE), v_raw, data, beta, rows_one)
+    )(blocks, exchange(pmsg, ("core", "x"), N_PLANE), v_raw, data, beta, rows_one)
     data_q, rmsg = call(
         products_kernel,
         [row4, (Z, BS)],

time: 123 us -> 123 us (level)
  no operation moved by 1% of the time
where the time goes in v7:
time: 123 us
  blocking collectives  100 us (81%)
  starting transfers between devices  15.8 us (13%)
  Pallas kernels  5.78 us (5%)
    all_to_all x5, blocking collectives, exchange(): lax.all_to_all(array.reshape(peers * n, 1, BS), axes, 0, 0, tiled=True)  78.1 us
    all_to_all x1, starting transfers between devices, exchange(): lax.all_to_all(array.reshape(peers * n, 1, BS), axes, 0, 0, tiled=True)  15.8 us
    all_gather x1, blocking collectives, on_device(): wanted = lax.all_gather(named, PLANE, axis=0, tiled=True)  14.1 us
    all_to_all x1, blocking collectives, exchange(): lax.all_to_all(array.reshape(peers, n, BS), axes, 0, 0, tiled=True)  8.2 us
    pallas_call x1, Pallas kernels, on_device(): call(first_kernel, [row4, zshape, (ENTRIES, BS)], [HBM] * 5, [msg, pltpu....  2.79 us
  transfers between devices with their start and end apart: 1, of which 0 were waited for; matrix products, arithmetic and copies ran while one was open for 0% of the time, Pallas kernels for 0%

profile of v7, /device:TPU:1, one launch (start us, length us, event | category | flops | bytes accessed | tf_op | source)
XLA Modules:
  0.0 122.6 jit_solution(14917743850820895088)
XLA Ops:
  0.6 0.0 copy-start
  0.6 2.8 %shard_map.68 = (f32[4,128]{1,0:T(4,128)}, f32[528,128]{1,0:T(8,128)}, f32[32,128]{1,0:T(8,128)}) custom-call(f32[4,8,128,128]{3,2,1,0:T(8,128)} %bitcast.29, f32[4,512]{1,0:T(4,128)} %seis.1, s32[4,512]{1,0:T(4,128)} %signs.1, s32[4,8]{1,0:T(4,128)} %pat.1, s32[2048]{0:T(1024)} %own.1), custom_call_target="tpu_custom_call" | custom-call | flops 1048576 | bytes 2097152 | tf_op jit(solution)/shard_map/pallas_call | solution.py:397
  3.4 15.8 %all-to-all-start = ((f32[528,1,128]{2,1,0:T(1,128)}), f32[528,1,128]{2,1,0:T(1,128)S(1)}, u32[]{:S(2)}, u32[]{:S(2)}) async-start(f32[528,1,128]{2,1,0:T(1,128)} %bitcast.46), calls=%async_computation | async-start | bytes 540672 | tf_op jit(solution)/shard_map/all_to_all | solution.py:377
  19.2 14.1 %all_gather.3.wanted = f32[256,128]{1,0:T(8,128)S(1)} all-gather(f32[32,128]{1,0:T(8,128)} %get-tuple-element.23), channel_id=1, replica_groups=mesh['x'=4,'z'=16,'core'=2,'y'=4] {'x','core'}, dimensions={0}, use_global_device_ids=true | all-gather | bytes 147456 | tf_op jit(solution)/shard_map/all_gather | solution.py:415
  33.3 0.0 all-to-all-done
  33.3 0.4 shard_map.69
  33.7 15.4 %all_to_all.35 = f32[392,1,128]{2,1,0:T(1,128)S(1)} all-to-all(f32[392,1,128]{2,1,0:T(1,128)S(1)} %bitcast.40), channel_id=1, replica_groups=mesh['x'=4,'z'=16,'core'=2,'y'=4] {'core','x'}, dimensions={0} | all-to-all | bytes 401408 | tf_op jit(solution)/shard_map/all_to_all | solution.py:377
  49.1 0.0 copy-done
  49.1 0.3 shard_map.70
  49.4 0.0 copy-start.1
  49.5 8.2 %all_to_all.36 = f32[4,8,128]{2,1,0:T(8,128)S(1)} all-to-all(f32[4,8,128]{2,1,0:T(8,128)S(1)} %bitcast.44), channel_id=1, replica_groups=mesh['x'=4,'z'=16,'core'=2,'y'=4] {'y'}, dimensions={0} | all-to-all | bytes 32768 | tf_op jit(solution)/shard_map/all_to_all | solution.py:376
  57.7 0.3 shard_map.71
  57.9 18.5 %all_to_all.37 = f32[528,1,128]{2,1,0:T(1,128)S(1)} all-to-all(f32[528,1,128]{2,1,0:T(1,128)S(1)} %bitcast.39), channel_id=1, replica_groups=mesh['x'=4,'z'=16,'core'=2,'y'=4] {'z'}, dimensions={0} | all-to-all | bytes 540672 | tf_op jit(solution)/shard_map/all_to_all | solution.py:377
  76.4 0.4 shard_map.72
  76.8 15.4 %all_to_all.38 = f32[392,1,128]{2,1,0:T(1,128)S(1)} all-to-all(f32[392,1,128]{2,1,0:T(1,128)S(1)} %bitcast.36), channel_id=1, replica_groups=mesh['x'=4,'z'=16,'core'=2,'y'=4] {'core','x'}, dimensions={0} | all-to-all | bytes 401408 | tf_op jit(solution)/shard_map/all_to_all | solution.py:377
  92.2 0.0 copy-done.1
  92.2 0.4 shard_map.73
  92.6 12.3 %all_to_all.39 = f32[384,1,128]{2,1,0:T(1,128)S(1)} all-to-all(f32[384,1,128]{2,1,0:T(1,128)S(1)} %bitcast.41), channel_id=1, replica_groups=mesh['x'=4,'z'=16,'core'=2,'y'=4] {'x','core','y'}, dimensions={0} | all-to-all | bytes 393216 | tf_op jit(solution)/shard_map/all_to_all | solution.py:377
  104.9 0.4 shard_map.74
  105.3 16.4 %all_to_all.40 = f32[16,1,128]{2,1,0:T(1,128)S(1)} all-to-all(f32[16,1,128]{2,1,0:T(1,128)S(1)} %bitcast.45), channel_id=1, replica_groups=mesh['x'=4,'z'=16,'core'=2,'y'=4] {'z'}, dimensions={0} | all-to-all | bytes 16384 | tf_op jit(solution)/shard_map/all_to_all | solution.py:377
  121.7 0.9 shard_map.75
Async XLA Ops:
  0.6 48.5 %copy-start = (f32[1,4,8,128,128]{4,3,2,1,0:T(8,128)S(1)}, f32[1,4,8,128,128]{4,3,2,1,0:T(8,128)}, u32[]{:S(2)}) copy-start(f32[1,4,8,128,128]{4,3,2,1,0:T(8,128)} %param.5) | copy-start | bytes 6291460
  3.4 29.9 %all-to-all-start = ((f32[528,1,128]{2,1,0:T(1,128)}), f32[528,1,128]{2,1,0:T(1,128)S(1)}, u32[]{:S(2)}, u32[]{:S(2)}) async-start(f32[528,1,128]{2,1,0:T(1,128)} %bitcast.46), calls=%async_computation | async-start | bytes 540672 | tf_op jit(solution)/shard_map/all_to_all | solution.py:377
  49.4 42.8 %copy-start.1 = (f32[4,128]{1,0:T(4,128)S(1)}, f32[4,128]{1,0:T(4,128)}, u32[]{:S(2)}) copy-start(f32[4,128]{1,0:T(4,128)} %get-tuple-element.29.data) | copy-start | bytes 6148

commit v8 on v7

--- a/solution.py
+++ b/solution.py
@@ -25,7 +25,7 @@
 ZCH = ENTRIES + 1
 PCH = WANT + 1
 PRODUCTS = 12
-PART = 4
+PART = 2
 GROUPS = BS // ENTRIES
 DOTS = 9
 

time: 123 us -> 123 us (level)
  no operation moved by 1% of the time
where the time goes in v8:
time: 123 us; the launch traced here: 122 us
  blocking collectives  100 us (81%)
  starting transfers between devices  15.8 us (13%)
  Pallas kernels  5.61 us (5%)
    all_to_all x5, blocking collectives, exchange(): lax.all_to_all(array.reshape(peers * n, 1, BS), axes, 0, 0, tiled=True)  78.1 us
    all_to_all x1, starting transfers between devices, exchange(): lax.all_to_all(array.reshape(peers * n, 1, BS), axes, 0, 0, tiled=True)  15.8 us
    all_gather x1, blocking collectives, on_device(): wanted = lax.all_gather(named, PLANE, axis=0, tiled=True)  14.1 us
    all_to_all x1, blocking collectives, exchange(): lax.all_to_all(array.reshape(peers, n, BS), axes, 0, 0, tiled=True)  8.19 us
    pallas_call x1, Pallas kernels, on_device(): call(first_kernel, [row4, zshape, (ENTRIES, BS)], [HBM] * 5, [msg, pltpu....  2.62 us
  transfers between devices with their start and end apart: 1, of which 0 were waited for; matrix products, arithmetic and copies ran while one was open for 0% of the time, Pallas kernels for 0%

profile of v8, /device:TPU:1, one launch (start us, length us, event | category | flops | bytes accessed | tf_op | source)
XLA Modules:
  0.0 122.5 jit_solution(9959008208294280145)
XLA Ops:
  0.6 0.0 copy-start
  0.6 2.6 %shard_map.68 = (f32[4,128]{1,0:T(4,128)}, f32[528,128]{1,0:T(8,128)}, f32[32,128]{1,0:T(8,128)}) custom-call(f32[4,8,128,128]{3,2,1,0:T(8,128)} %bitcast.29, f32[4,512]{1,0:T(4,128)} %seis.1, s32[4,512]{1,0:T(4,128)} %signs.1, s32[4,8]{1,0:T(4,128)} %pat.1, s32[2048]{0:T(1024)} %own.1), custom_call_target="tpu_custom_call" | custom-call | flops 1048576 | bytes 2097152 | tf_op jit(solution)/shard_map/pallas_call | solution.py:397
  3.3 15.8 %all-to-all-start = ((f32[528,1,128]{2,1,0:T(1,128)}), f32[528,1,128]{2,1,0:T(1,128)S(1)}, u32[]{:S(2)}, u32[]{:S(2)}) async-start(f32[528,1,128]{2,1,0:T(1,128)} %bitcast.46), calls=%async_computation | async-start | bytes 540672 | tf_op jit(solution)/shard_map/all_to_all | solution.py:377
  19.0 14.1 %all_gather.3.wanted = f32[256,128]{1,0:T(8,128)S(1)} all-gather(f32[32,128]{1,0:T(8,128)} %get-tuple-element.23), channel_id=1, replica_groups=mesh['x'=4,'z'=16,'core'=2,'y'=4] {'x','core'}, dimensions={0}, use_global_device_ids=true | all-gather | bytes 147456 | tf_op jit(solution)/shard_map/all_gather | solution.py:415
  33.1 0.0 all-to-all-done
  33.1 0.4 shard_map.69
  33.5 15.4 %all_to_all.35 = f32[392,1,128]{2,1,0:T(1,128)S(1)} all-to-all(f32[392,1,128]{2,1,0:T(1,128)S(1)} %bitcast.40), channel_id=1, replica_groups=mesh['x'=4,'z'=16,'core'=2,'y'=4] {'core','x'}, dimensions={0} | all-to-all | bytes 401408 | tf_op jit(solution)/shard_map/all_to_all | solution.py:377
  49.0 0.0 copy-done
  49.0 0.3 shard_map.70
  49.3 0.0 copy-start.1
  49.3 8.2 %all_to_all.36 = f32[4,8,128]{2,1,0:T(8,128)S(1)} all-to-all(f32[4,8,128]{2,1,0:T(8,128)S(1)} %bitcast.44), channel_id=1, replica_groups=mesh['x'=4,'z'=16,'core'=2,'y'=4] {'y'}, dimensions={0} | all-to-all | bytes 32768 | tf_op jit(solution)/shard_map/all_to_all | solution.py:376
  57.5 0.3 shard_map.71
  57.7 18.5 %all_to_all.37 = f32[528,1,128]{2,1,0:T(1,128)S(1)} all-to-all(f32[528,1,128]{2,1,0:T(1,128)S(1)} %bitcast.39), channel_id=1, replica_groups=mesh['x'=4,'z'=16,'core'=2,'y'=4] {'z'}, dimensions={0} | all-to-all | bytes 540672 | tf_op jit(solution)/shard_map/all_to_all | solution.py:377
  76.3 0.4 shard_map.72
  76.6 15.4 %all_to_all.38 = f32[392,1,128]{2,1,0:T(1,128)S(1)} all-to-all(f32[392,1,128]{2,1,0:T(1,128)S(1)} %bitcast.36), channel_id=1, replica_groups=mesh['x'=4,'z'=16,'core'=2,'y'=4] {'core','x'}, dimensions={0} | all-to-all | bytes 401408 | tf_op jit(solution)/shard_map/all_to_all | solution.py:377
  92.1 0.0 copy-done.1
  92.1 0.4 shard_map.73
  92.4 12.3 %all_to_all.39 = f32[384,1,128]{2,1,0:T(1,128)S(1)} all-to-all(f32[384,1,128]{2,1,0:T(1,128)S(1)} %bitcast.41), channel_id=1, replica_groups=mesh['x'=4,'z'=16,'core'=2,'y'=4] {'x','core','y'}, dimensions={0} | all-to-all | bytes 393216 | tf_op jit(solution)/shard_map/all_to_all | solution.py:377
  104.7 0.4 shard_map.74
  105.1 16.4 %all_to_all.40 = f32[16,1,128]{2,1,0:T(1,128)S(1)} all-to-all(f32[16,1,128]{2,1,0:T(1,128)S(1)} %bitcast.45), channel_id=1, replica_groups=mesh['x'=4,'z'=16,'core'=2,'y'=4] {'z'}, dimensions={0} | all-to-all | bytes 16384 | tf_op jit(solution)/shard_map/all_to_all | solution.py:377
  121.6 0.9 shard_map.75
Async XLA Ops:
  0.6 48.3 %copy-start = (f32[1,4,8,128,128]{4,3,2,1,0:T(8,128)S(1)}, f32[1,4,8,128,128]{4,3,2,1,0:T(8,128)}, u32[]{:S(2)}) copy-start(f32[1,4,8,128,128]{4,3,2,1,0:T(8,128)} %param.5) | copy-start | bytes 6291460
  3.3 29.9 %all-to-all-start = ((f32[528,1,128]{2,1,0:T(1,128)}), f32[528,1,128]{2,1,0:T(1,128)S(1)}, u32[]{:S(2)}, u32[]{:S(2)}) async-start(f32[528,1,128]{2,1,0:T(1,128)} %bitcast.46), calls=%async_computation | async-start | bytes 540672 | tf_op jit(solution)/shard_map/all_to_all | solution.py:377
  49.3 42.8 %copy-start.1 = (f32[4,128]{1,0:T(4,128)S(1)}, f32[4,128]{1,0:T(4,128)}, u32[]{:S(2)}) copy-start(f32[4,128]{1,0:T(4,128)} %get-tuple-element.29.data) | copy-start | bytes 6148
